TPU v7x, 128 devices: a whole 4x4x4 slice. The times are simulated.
128 devices in a mesh: dp: 2 (over z_lo), fsdp: 64 (over y, z_hi, x, core).
Axes of the slice: x: 4, y: 4, z: 4 (z_hi: 2, z_lo: 2; z = z_hi * 2 + z_lo), core: 2. Of those that a mesh axis runs over, the one named last changes fastest.
Arguments:
- tokens: bfloat16 [256, 64, 2048], P(('dp', 'fsdp')), may hold values from -6 to 6
- segments: int32 [256, 64], P(('dp', 'fsdp')), may hold values from 0 to 7, never falling along the last dimension, each value on 1 to 32 neighbouring positions
- qkv_weight: bfloat16 [2048, 4096], P('fsdp'), may hold values from -0.125 to 0.125
- out_weight: bfloat16 [2048, 2048], P('fsdp'), may hold values from -0.25 to 0.25
- attn_gain: bfloat16 [2048], P('fsdp'), may hold values from 0.25 to 1.75
- query_gain: bfloat16 [128], P('fsdp'), may hold values from 0.25 to 1.75
- key_gain: bfloat16 [128], P('fsdp'), may hold values from 0.25 to 1.75
- ffn_weight: bfloat16 [2048, 12288], P('fsdp'), may hold values from -0.125 to 0.125
- down_weight: bfloat16 [6144, 2048], P('fsdp'), may hold values from -0.078125 to 0.078125
- ffn_gain: bfloat16 [2048], P('fsdp'), may hold values from 0.25 to 1.75
- out_grad: bfloat16 [256, 64, 2048], P(('dp', 'fsdp')), may hold values from -6 to 6
Outputs:
- result: bfloat16 [256, 64, 2048], P(('dp', 'fsdp'))
- tokens_grad: float32 [256, 64, 2048], P(('dp', 'fsdp'))
- qkv_weight_grad: float32 [2048, 4096], P('fsdp')
- out_weight_grad: float32 [2048, 2048], P('fsdp')
- attn_gain_grad: float32 [2048], P('fsdp')
- query_gain_grad: float32 [128], P('fsdp')
- key_gain_grad: float32 [128], P('fsdp')
- ffn_weight_grad: float32 [2048, 12288], P('fsdp')
- down_weight_grad: float32 [6144, 2048], P('fsdp')
- ffn_gain_grad: float32 [2048], P('fsdp')
Inputs may be any that keep to these rules, and one draw needn't show every extreme that they name: `segments`: within each sequence the segment numbers never fall; every document holds 1 to 32 tokens, and one holds exactly 32.
All inputs are finite; a program needn't handle non-finite values.
Results may differ from a plain program's by a relative error of at most 0.024.
Values may be sent and summed in bfloat16 or wider, within the bound.
No kernel may reach another device: no remote copies, remote signals or barrier semaphores. Data moves between devices by JAX's collectives and lax.ppermute only.
A program may use at most 512 MiB of HBM per device.

v0:
```python
import jax
import jax.numpy as jnp
from jax import lax
from jax.sharding import PartitionSpec as P

D = 2048
H = 16
KVH = 8
HD = 128
FF = 6144


epsilon = 1e-06
neg_large = -1e30
rope_base = 1000000.0


def normed(values, gain_vec):
    return (
        values * lax.rsqrt(jnp.mean(values * values, axis=-1, keepdims=True) + epsilon) * gain_vec
    )


def norm_backward(values, gain_vec, grad_norm):
    inv_root = lax.rsqrt(jnp.mean(values * values, axis=-1, keepdims=True) + epsilon)
    plain_norm = values * inv_root
    grad_plain = grad_norm * gain_vec
    grad_values = inv_root * (
        grad_plain - plain_norm * jnp.mean(grad_plain * plain_norm, axis=-1, keepdims=True)
    )
    return (grad_values, grad_norm * plain_norm)


def doc_positions(segments):
    length = segments.shape[-1]
    places = jnp.arange(length, dtype=jnp.int32)
    starts = jnp.concatenate(
        [jnp.ones(segments.shape[:-1] + (1,), jnp.bool_), segments[..., 1:] != segments[..., :-1]],
        axis=-1,
    )
    first_place = lax.cummax(jnp.where(starts, places, 0), axis=segments.ndim - 1)
    return places - first_place


def rope_tables(positions, head_dim):
    half_dim = head_dim // 2
    frequency = rope_base ** (-(jnp.arange(half_dim, dtype=jnp.float32) * 2.0 / head_dim))
    angles = positions.astype(jnp.float32)[..., None] * frequency
    angles = jnp.concatenate([angles, angles], axis=-1)
    return (jnp.cos(angles), jnp.sin(angles))


def rotate(values, cosine, sine_table):
    half_dim = values.shape[-1] // 2
    turned = jnp.concatenate([-values[..., half_dim:], values[..., :half_dim]], axis=-1)
    return values * cosine + turned * sine_table


def unrotate(values, cosine, sine_table):
    half_dim = values.shape[-1] // 2
    scaled = values * sine_table
    back_part = jnp.concatenate([scaled[..., half_dim:], -scaled[..., :half_dim]], axis=-1)
    return values * cosine + back_part


def contract_last(left_side, right_side):
    return lax.dot_general(
        left_side, right_side, (((1,), (1,)), ((), ())), preferred_element_type=jnp.float32
    )


def contract_first(left_side, right_side):
    return lax.dot_general(
        left_side, right_side, (((0,), (0,)), ((), ())), preferred_element_type=jnp.float32
    )


def attn_fetch(qkv_weight, out_weight, attn_gain, query_gain, key_gain):
    return (
        lax.all_gather(qkv_weight, "fsdp", axis=0, tiled=True),
        lax.all_gather(out_weight, "fsdp", axis=0, tiled=True),
        lax.all_gather(attn_gain, "fsdp", axis=0, tiled=True),
        lax.all_gather(query_gain, "fsdp", axis=0, tiled=True),
        lax.all_gather(key_gain, "fsdp", axis=0, tiled=True),
    )


def ffn_fetch(ffn_weight, down_weight, ffn_gain):
    return (
        lax.all_gather(ffn_weight, "fsdp", axis=0, tiled=True),
        lax.all_gather(down_weight, "fsdp", axis=0, tiled=True),
        lax.all_gather(ffn_gain, "fsdp", axis=0, tiled=True),
    )


def head_values(qkv_proj, seg_row, gain_query, gain_key):
    length = qkv_proj.shape[0]
    queries = qkv_proj[:, : H * HD].reshape(length, H, HD)
    key_part = qkv_proj[:, H * HD : (H + KVH) * HD].reshape(length, KVH, HD)
    value_part = qkv_proj[:, (H + KVH) * HD :].reshape(length, KVH, HD)
    cosine, sine_table = rope_tables(doc_positions(seg_row), HD)
    cosine = cosine[:, None, :]
    sine_table = sine_table[:, None, :]
    query_rot = rotate(normed(queries, gain_query), cosine, sine_table).astype(jnp.bfloat16)
    key_rot = rotate(normed(key_part, gain_key), cosine, sine_table).astype(jnp.bfloat16)
    return (
        queries,
        key_part,
        value_part.astype(jnp.bfloat16),
        query_rot,
        key_rot,
        cosine,
        sine_table,
    )


def masked_scores(query_rot, key_rot, seg_row):
    length = query_rot.shape[0]
    grouped = query_rot.reshape(length, KVH, H // KVH, HD)
    scores = jnp.einsum(
        "ahgd,bhd->hgab", grouped, key_rot, preferred_element_type=jnp.float32
    ) * HD ** (-0.5)
    places = jnp.arange(length)
    allowed = (seg_row[:, None] == seg_row[None, :]) & (places[None, :] <= places[:, None])
    return jnp.where(allowed[None, None], scores, neg_large)


def attend_forward(inputs, seg_row, attn_set):
    qkv_full, out_full, gain_in, gain_query, gain_key = attn_set
    length = inputs.shape[0]
    normal_in = normed(inputs, gain_in.astype(jnp.float32)).astype(jnp.bfloat16)
    qkv_proj = jnp.dot(normal_in, qkv_full, preferred_element_type=jnp.float32)
    queries, key_part, value_low, query_rot, key_rot, cosine, sine_table = head_values(
        qkv_proj, seg_row, gain_query.astype(jnp.float32), gain_key.astype(jnp.float32)
    )
    scores = masked_scores(query_rot, key_rot, seg_row)
    peak_score = jnp.max(scores, axis=-1, keepdims=True)
    exp_scores = jnp.exp(scores - peak_score)
    exp_total = jnp.sum(exp_scores, axis=-1, keepdims=True)
    probabilities = (exp_scores / exp_total).astype(jnp.bfloat16)
    log_total = peak_score + jnp.log(exp_total)
    mixed_heads = jnp.einsum(
        "hgab,bhd->ahgd", probabilities, value_low, preferred_element_type=jnp.float32
    )
    mixed_heads = mixed_heads.reshape(length, H * HD).astype(jnp.bfloat16)
    hidden = inputs + jnp.dot(mixed_heads, out_full, preferred_element_type=jnp.float32)
    return (hidden, normal_in, qkv_proj, log_total, mixed_heads)


def attend_backward(inputs, seg_row, qkv_proj, log_total, attn_set, grad_hidden):
    qkv_full, out_full, gain_in, gain_query, gain_key = attn_set
    length = inputs.shape[0]
    gain_query = gain_query.astype(jnp.float32)
    gain_key = gain_key.astype(jnp.float32)
    grad_hidden_low = grad_hidden.astype(jnp.bfloat16)
    grad_mixed = (
        contract_last(grad_hidden_low, out_full)
        .astype(jnp.bfloat16)
        .reshape(length, KVH, H // KVH, HD)
    )
    queries, key_part, value_low, query_rot, key_rot, cosine, sine_table = head_values(
        qkv_proj, seg_row, gain_query, gain_key
    )
    scores = masked_scores(query_rot, key_rot, seg_row)
    soft_full = jnp.exp(scores - log_total)
    grad_probs = jnp.einsum(
        "ahgd,bhd->hgab", grad_mixed, value_low, preferred_element_type=jnp.float32
    )
    row_delta = jnp.sum(soft_full * grad_probs, axis=-1, keepdims=True)
    grad_scores = (soft_full * (grad_probs - row_delta)).astype(jnp.bfloat16)
    grouped = query_rot.reshape(length, KVH, H // KVH, HD)
    grad_query_rot = jnp.einsum(
        "hgab,bhd->ahgd", grad_scores, key_rot, preferred_element_type=jnp.float32
    ) * HD ** (-0.5)
    grad_key_rot = jnp.einsum(
        "hgab,ahgd->bhd", grad_scores, grouped, preferred_element_type=jnp.float32
    ) * HD ** (-0.5)
    grad_value = jnp.einsum(
        "hgab,ahgd->bhd",
        soft_full.astype(jnp.bfloat16),
        grad_mixed,
        preferred_element_type=jnp.float32,
    )
    grad_query_rot = grad_query_rot.reshape(length, H, HD)
    grad_queries, query_terms = norm_backward(
        queries, gain_query, unrotate(grad_query_rot, cosine, sine_table)
    )
    grad_keys, key_terms = norm_backward(
        key_part, gain_key, unrotate(grad_key_rot, cosine, sine_table)
    )
    grad_qkv = jnp.concatenate(
        [
            grad_queries.reshape(length, H * HD),
            grad_keys.reshape(length, KVH * HD),
            grad_value.reshape(length, KVH * HD),
        ],
        axis=-1,
    ).astype(jnp.bfloat16)
    grad_normal = contract_last(grad_qkv, qkv_full)
    grad_inputs, attn_terms = norm_backward(inputs, gain_in.astype(jnp.float32), grad_normal)
    gain_parts = (
        jnp.sum(attn_terms, axis=0),
        jnp.sum(query_terms, axis=(0, 1)),
        jnp.sum(key_terms, axis=(0, 1)),
    )
    return (grad_hidden + grad_inputs, gain_parts, grad_hidden_low, grad_qkv)


def ffn_forward(hidden, ffn_set):
    ffn_full, down_full, gain_mid = ffn_set
    normal_mid = normed(hidden, gain_mid.astype(jnp.float32)).astype(jnp.bfloat16)
    gate_up = jnp.dot(normal_mid, ffn_full, preferred_element_type=jnp.float32)
    gate_part = gate_up[:, :FF]
    upward = gate_up[:, FF:]
    active = (gate_part * jax.nn.sigmoid(gate_part) * upward).astype(jnp.bfloat16)
    outcome = hidden + jnp.dot(active, down_full, preferred_element_type=jnp.float32)
    return (outcome, normal_mid, gate_up, active)


def ffn_backward(hidden, gate_up, ffn_set, grad_result):
    ffn_full, down_full, gain_mid = ffn_set
    grad_out_low = grad_result.astype(jnp.bfloat16)
    grad_active = contract_last(grad_out_low, down_full)
    gate_part = gate_up[:, :FF]
    upward = gate_up[:, FF:]
    sig_gate = jax.nn.sigmoid(gate_part)
    grad_gate = grad_active * upward * sig_gate * (1.0 + gate_part * (1.0 - sig_gate))
    grad_upward = grad_active * gate_part * sig_gate
    grad_gate_up = jnp.concatenate([grad_gate, grad_upward], axis=-1).astype(jnp.bfloat16)
    grad_normal = contract_last(grad_gate_up, ffn_full)
    grad_from_norm, gain_terms = norm_backward(hidden, gain_mid.astype(jnp.float32), grad_normal)
    return (grad_result + grad_from_norm, jnp.sum(gain_terms, axis=0), grad_out_low, grad_gate_up)


def on_device(
    tokens,
    segments,
    qkv_weight,
    out_weight,
    attn_gain,
    query_gain,
    key_gain,
    ffn_weight,
    down_weight,
    ffn_gain,
    out_grad,
):
    micros = tokens.shape[0]
    attn_set = None
    ffn_set = None
    saved = []
    outputs = []
    for micro_index in range(micros):
        attn_set = attn_fetch(qkv_weight, out_weight, attn_gain, query_gain, key_gain)
        inputs = tokens[micro_index].astype(jnp.float32)
        hidden, normal_in, qkv_proj, log_total, mixed_heads = attend_forward(
            inputs, segments[micro_index], attn_set
        )
        ffn_set = ffn_fetch(ffn_weight, down_weight, ffn_gain)
        outcome, normal_mid, gate_up, active = ffn_forward(hidden, ffn_set)
        outputs.append(outcome.astype(jnp.bfloat16))
        saved.append(
            (normal_in, qkv_proj, log_total, mixed_heads, hidden, normal_mid, gate_up, active)
        )
    input_grads = []
    kept_normal_in = []
    kept_grad_qkv = []
    kept_mixed = []
    kept_hidden_low = []
    kept_normal_mid = []
    kept_gate_up = []
    kept_active = []
    kept_out_low = []
    attn_gain_total = jnp.zeros((D,), jnp.float32)
    query_total = jnp.zeros((HD,), jnp.float32)
    key_total = jnp.zeros((HD,), jnp.float32)
    ffn_gain_total = jnp.zeros((D,), jnp.float32)
    for micro_index in range(micros):
        ffn_set = ffn_fetch(ffn_weight, down_weight, ffn_gain)
        normal_in, qkv_proj, log_total, mixed_heads, hidden, normal_mid, gate_up, active = saved[
            micro_index
        ]
        grad_result = out_grad[micro_index].astype(jnp.float32)
        grad_hidden, ffn_gain_part, grad_out_low, grad_gate_up = ffn_backward(
            hidden, gate_up, ffn_set, grad_result
        )
        attn_set = attn_fetch(qkv_weight, out_weight, attn_gain, query_gain, key_gain)
        inputs = tokens[micro_index].astype(jnp.float32)
        grad_inputs, gain_parts, grad_hidden_low, grad_qkv = attend_backward(
            inputs, segments[micro_index], qkv_proj, log_total, attn_set, grad_hidden
        )
        input_grads.append(grad_inputs)
        attn_gain_total = attn_gain_total + gain_parts[0]
        query_total = query_total + gain_parts[1]
        key_total = key_total + gain_parts[2]
        ffn_gain_total = ffn_gain_total + ffn_gain_part
        kept_normal_in.append(normal_in)
        kept_grad_qkv.append(grad_qkv)
        kept_mixed.append(mixed_heads)
        kept_hidden_low.append(grad_hidden_low)
        kept_normal_mid.append(normal_mid)
        kept_gate_up.append(grad_gate_up)
        kept_active.append(active)
        kept_out_low.append(grad_out_low)
    normal_in_all = jnp.concatenate(kept_normal_in, axis=0)
    grad_qkv_all = jnp.concatenate(kept_grad_qkv, axis=0)
    mixed_all = jnp.concatenate(kept_mixed, axis=0)
    hidden_low_all = jnp.concatenate(kept_hidden_low, axis=0)
    normal_mid_all = jnp.concatenate(kept_normal_mid, axis=0)
    gate_up_all = jnp.concatenate(kept_gate_up, axis=0)
    active_all = jnp.concatenate(kept_active, axis=0)
    out_low_all = jnp.concatenate(kept_out_low, axis=0)
    qkv_term = contract_first(normal_in_all, grad_qkv_all)
    out_term = contract_first(mixed_all, hidden_low_all)
    attn_shards = (
        lax.psum_scatter(qkv_term, "fsdp", scatter_dimension=0, tiled=True),
        lax.psum_scatter(out_term, "fsdp", scatter_dimension=0, tiled=True),
        lax.psum_scatter(attn_gain_total, "fsdp", scatter_dimension=0, tiled=True),
        lax.psum_scatter(query_total, "fsdp", scatter_dimension=0, tiled=True),
        lax.psum_scatter(key_total, "fsdp", scatter_dimension=0, tiled=True),
        lax.psum_scatter(ffn_gain_total, "fsdp", scatter_dimension=0, tiled=True),
    )
    columns_in = normal_mid_all
    ffn_shard = lax.psum_scatter(
        contract_first(columns_in, gate_up_all), "fsdp", scatter_dimension=0, tiled=True
    )
    columns_in = active_all
    down_shard = lax.psum_scatter(
        contract_first(columns_in, out_low_all), "fsdp", scatter_dimension=0, tiled=True
    )
    summed = (
        lax.psum(attn_shards[0].astype(jnp.bfloat16), "dp").astype(jnp.float32),
        lax.psum(attn_shards[1].astype(jnp.bfloat16), "dp").astype(jnp.float32),
        lax.psum(attn_shards[2].astype(jnp.bfloat16), "dp").astype(jnp.float32),
        lax.psum(attn_shards[3].astype(jnp.bfloat16), "dp").astype(jnp.float32),
        lax.psum(attn_shards[4].astype(jnp.bfloat16), "dp").astype(jnp.float32),
        lax.psum(ffn_shard.astype(jnp.bfloat16), "dp").astype(jnp.float32),
        lax.psum(down_shard.astype(jnp.bfloat16), "dp").astype(jnp.float32),
        lax.psum(attn_shards[5].astype(jnp.bfloat16), "dp").astype(jnp.float32),
    )
    return (
        jnp.stack(outputs, axis=0),
        jnp.stack(input_grads, axis=0),
        summed[0],
        summed[1],
        summed[2],
        summed[3],
        summed[4],
        summed[5],
        summed[6],
        summed[7],
    )


def solution(mesh):
    placed = (
        P(("dp", "fsdp"), None, None),
        P(("dp", "fsdp"), None),
        P("fsdp", None),
        P("fsdp", None),
        P("fsdp"),
        P("fsdp"),
        P("fsdp"),
        P("fsdp", None),
        P("fsdp", None),
        P("fsdp"),
        P(("dp", "fsdp"), None, None),
    )
    return jax.shard_map(
        on_device,
        mesh=mesh,
        in_specs=placed,
        out_specs=(
            P(("dp", "fsdp"), None, None),
            P(("dp", "fsdp"), None, None),
            P("fsdp", None),
            P("fsdp", None),
            P("fsdp"),
            P("fsdp"),
            P("fsdp"),
            P("fsdp", None),
            P("fsdp", None),
            P("fsdp"),
        ),
        check_vma=False,
    )
```

profile of v0, /device:TPU:0, one launch (start us, length us, event | category | flops | bytes accessed | tf_op | source)
XLA Modules:
  0.0 2647.8 jit_solution(7380942622352458773)
XLA Ops:
  16.1 176.6 %all-reduce.9 = (bf16[2048]{0:T(1024)(128)(2,1)S(1)}, bf16[128]{0:T(256)(128)(2,1)S(1)}, bf16[128]{0:T(256)(128)(2,1)S(1)}, bf16[2048]{0:T(1024)(128)(2,1)S(1)}) all-reduce(bf16[2048]{0:T(1024)(128)(2,1)S(1)} %dynamic-update-slice, bf16[128]{0:T(256)(128)(2,1)S(1)} %dynamic-update-slice.1, ...), channel_id=1, replica_groups=mesh['dp'=2,'fsdp'=64] {'fsdp'}, use_global_device_ids=true, to_apply=%add | all-reduce | flops 4352 | bytes 17408
  200.1 9.4 fusion.167
  211.2 9.1 fusion.169
  223.2 1.4 copy.230
  228.6 1.4 copy.241
  232.7 2.2 multiply_multiply_fusion.1
  237.1 2.3 reshape.605
  241.5 2.4 reshape.609
  251.3 5.3 multiply_reduce_fusion.12
  257.3 1.7 multiply_reduce_fusion.10
  259.2 158.2 %all-gather.9.cloned.1.call-done = bf16[2048,12288]{1,0:T(8,128)(2,1)} async-done(((bf16[32,12288]{1,0:T(8,128)(2,1)}), bf16[2048,12288]{1,0:T(8,128)(2,1)}) %all-gather.9.cloned.1.call-update) | async-done | bytes 50331664 | tf_op jit(solution)/shard_map/all_gather | solution.py:90
  417.3 21.8 fusion.168
  439.2 110.4 %all-gather.11.cloned.1.call-done = bf16[6144,2048]{1,0:T(8,128)(2,1)} async-done(((bf16[96,2048]{1,0:T(8,128)(2,1)}), bf16[6144,2048]{1,0:T(8,128)(2,1)}) %all-gather.11.cloned.1.call-update) | async-done | bytes 25165840 | tf_op jit(solution)/shard_map/all_gather | solution.py:91
  549.5 14.0 multiply_convert_fusion.3
  563.6 22.9 multiply_reduce_fusion.1
  586.4 21.8 fusion.170
  608.2 14.2 multiply_convert_fusion.1
  622.4 22.8 multiply_reduce_fusion
  645.3 1.6 fusion.156
  647.7 8.2 fusion.97
  657.2 6.1 convolution_convert_fusion
  663.8 6.0 convolution_convert_fusion.1
  677.7 1.6 multiply_reduce_fusion.3
  680.1 2.3 reshape.612
  683.7 2.3 reshape.617
  694.2 2.2 fusion.76
  697.1 14.4 fusion.34
  712.7 19.7 fusion.20
  733.9 36.4 %fusion = f32[2048,12288]{1,0:T(8,128)} fusion(bf16[64,6144]{1,0:T(8,128)(2,1)} %get-tuple-element.51, bf16[64,6144]{1,0:T(8,128)(2,1)} %get-tuple-element.50, bf16[64,6144]{1,0:T(8,128)(2,1)S(1)} %copy-done.10, bf16[64,6144]{1,0:T(8,128)(2,1)S(1)} %copy-done.9, bf16[64,2048]{1,0:T(8,128)(2,1)S(1)} %copy-done.40, bf16[64,2048]{1,0:T(8,128)(2,1)S(1)} %copy-done.42), kind=kOutput, calls=%fused_computation | convolution fusion | flops 6456082432 | bytes 104333312 | tf_op jit(solution)/shard_map/dot_general | solution.py:73
  772.0 11.1 fusion.88
  783.2 12.2 fusion.60
  795.4 13.7 fusion.10
  809.1 11.6 fusion.11
  820.8 193.4 %reduce-scatter.7.cloned.1.call-done = f32[32,2048]{1,0:T(8,128)} async-done(((f32[2048,2048]{1,0:T(8,128)}), f32[32,2048]{1,0:T(8,128)}) %reduce-scatter.7.cloned.1.call-update) | async-done | bytes 262160 | tf_op jit(solution)/shard_map/reduce_scatter | solution.py:317
  1014.1 1.6 convert_element_type.258
  1015.8 383.8 %reduce-scatter.5.cloned.1.call-done = f32[32,4096]{1,0:T(8,128)} async-done(((f32[2048,4096]{1,0:T(8,128)}), f32[32,4096]{1,0:T(8,128)}) %reduce-scatter.5.cloned.1.call-update) | async-done | bytes 524304 | tf_op jit(solution)/shard_map/reduce_scatter | solution.py:316
  1399.6 1.8 convert_element_type.256
  1401.4 334.3 %reduce-scatter.11.cloned.1.call-done = f32[96,2048]{1,0:T(8,128)} async-done(((f32[6144,2048]{1,0:T(8,128)}), f32[96,2048]{1,0:T(8,128)}) %reduce-scatter.11.cloned.1.call-update) | async-done | bytes 786448 | tf_op jit(solution)/shard_map/reduce_scatter | solution.py:328
  1735.7 1.9 convert_element_type.268
  1737.6 556.7 %reduce-scatter.9.cloned.1.call-done = f32[32,12288]{1,0:T(8,128)} async-done(((f32[2048,12288]{1,0:T(8,128)}), f32[32,12288]{1,0:T(8,128)}) %reduce-scatter.9.cloned.1.call-update) | async-done | bytes 1572880 | tf_op jit(solution)/shard_map/reduce_scatter | solution.py:324
  2294.3 2.4 convert_element_type.266
  2296.8 325.3 %all-reduce.8 = (bf16[2048]{0:T(1024)(128)(2,1)S(1)}, bf16[128]{0:T(256)(128)(2,1)S(1)}, bf16[128]{0:T(256)(128)(2,1)S(1)}, bf16[2048]{0:T(1024)(128)(2,1)S(1)}) all-reduce(f32[2048]{0:T(1024)S(1)} %add.250, f32[128]{0:T(128)S(1)} %add.251, f32[128]{0:T(128)S(1)} %add.252, ...), channel_id=4, replica_groups=mesh['dp'=2,'fsdp'=64] {'fsdp'}, use_global_device_ids=true, to_apply=%region_30.31.clone | all-reduce | flops 4352 | bytes 26112
  2622.4 4.9 all-reduce.10
  2629.4 1.8 pad_maximum_fusion.1
  2631.2 1.4 fusion.67
  2634.1 1.8 convert_element_type.257
  2635.9 1.6 convert_element_type.259
  2637.5 2.4 convert_element_type.267
  (443 shorter events, 66.5 us)
Async XLA Ops:
  7.2 192.7 %copy-start.5 = (bf16[2,64,2048]{2,1,0:T(8,128)(2,1)S(1)}, bf16[2,64,2048]{2,1,0:T(8,128)(2,1)}, u32[]{:S(2)}) copy-start(bf16[2,64,2048]{2,1,0:T(8,128)(2,1)} %param.11) | copy-start | bytes 1572868
  7.2 192.9 %all-gather.5.cloned.1.call-start = ((), (), s32[]{:S(2)}) async-start(), calls=%async_computation.4 | async-start | bytes 17039360 | tf_op jit(solution)/shard_map/all_gather | solution.py:80
  7.9 243.4 %all-gather.7.cloned.1.call-start = ((), (), s32[]{:S(2)}) async-start(), calls=%async_computation.5 | async-start | bytes 8519680 | tf_op jit(solution)/shard_map/all_gather | solution.py:81
  8.7 408.7 %all-gather.9.cloned.1.call-start = ((), (), s32[]{:S(2)}) async-start(), calls=%async_computation.6 | async-start | bytes 51118080 | tf_op jit(solution)/shard_map/all_gather | solution.py:90
  9.4 540.1 %all-gather.11.cloned.1.call-start = ((), (), s32[]{:S(2)}) async-start(), calls=%async_computation.7 | async-start | bytes 25559040 | tf_op jit(solution)/shard_map/all_gather | solution.py:91
  10.0 1004.2 %reduce-scatter.7.cloned.1.call-start = ((), (), s32[]{:S(2)}) async-start(), calls=%async_computation.9 | async-start | bytes 17039360 | tf_op jit(solution)/shard_map/reduce_scatter | solution.py:317
  192.7 16.8 copy-start.98
  195.3 449.9 %copy-start.89 = (f32[2048]{0:T(1024)}, f32[2048]{0:T(1024)S(1)}, u32[]{:S(2)}) copy-start(f32[2048]{0:T(1024)S(1)} %convert_element_type.228) | copy-start | bytes 24580
  196.2 50.8 %copy-start.78 = (f32[64,128]{1,0:T(8,128)}, f32[64,128]{1,0:T(8,128)S(1)}, u32[]{:S(2)}) copy-start(f32[64,128]{1,0:T(8,128)S(1)} %get-tuple-element.91) | copy-start | bytes 98308
  196.2 50.8 %copy-start.82 = (f32[64,128]{1,0:T(8,128)}, f32[64,128]{1,0:T(8,128)S(1)}, u32[]{:S(2)}) copy-start(f32[64,128]{1,0:T(8,128)S(1)} %get-tuple-element.90) | copy-start | bytes 98308
  197.1 52.4 %copy-start.80 = (f32[64,128]{1,0:T(8,128)}, f32[64,128]{1,0:T(8,128)S(1)}, u32[]{:S(2)}) copy-start(f32[64,128]{1,0:T(8,128)S(1)} %get-tuple-element.87) | copy-start | bytes 98308
  197.1 52.4 %copy-start.84 = (f32[64,128]{1,0:T(8,128)}, f32[64,128]{1,0:T(8,128)S(1)}, u32[]{:S(2)}) copy-start(f32[64,128]{1,0:T(8,128)S(1)} %get-tuple-element.86) | copy-start | bytes 98308
  200.0 11.2 copy-start.38
  209.5 39.7 %copy-start.11 = (f32[64,4096]{1,0:T(8,128)}, f32[64,4096]{1,0:T(8,128)S(1)}, u32[]{:S(2)}) copy-start(f32[64,4096]{1,0:T(8,128)S(1)} %fusion.167) | copy-start | bytes 3145732
  220.4 23.6 copy-start.13
  220.4 25.1 copy-start.28
  256.7 388.6 %copy-start.3 = (f32[64,2048]{1,0:T(8,128)}, f32[64,2048]{1,0:T(8,128)S(1)}, u32[]{:S(2)}) copy-start(f32[64,2048]{1,0:T(8,128)S(1)} %get-tuple-element.117) | copy-start | bytes 1572868
  257.3 388.0 %copy-start.127 = (f32[64]{0:T(128)}, f32[64]{0:T(128)S(1)}, u32[]{:S(2)}) copy-start(f32[64]{0:T(128)S(1)} %add_rsqrt_fusion.6) | copy-start | bytes 772
  259.0 386.3 %copy-start.1 = (f32[64,2048]{1,0:T(8,128)}, f32[64,2048]{1,0:T(8,128)S(1)}, u32[]{:S(2)}) copy-start(f32[64,2048]{1,0:T(8,128)S(1)} %get-tuple-element.119) | copy-start | bytes 1572868
  259.0 386.3 %copy-start.125 = (f32[64]{0:T(128)}, f32[64]{0:T(128)S(1)}, u32[]{:S(2)}) copy-start(f32[64]{0:T(128)S(1)} %add_rsqrt_fusion.4) | copy-start | bytes 772
  259.1 180.0 %copy-start.41 = (bf16[64,2048]{1,0:T(8,128)(2,1)}, bf16[64,2048]{1,0:T(8,128)(2,1)S(1)}, u32[]{:S(2)}) copy-start(bf16[64,2048]{1,0:T(8,128)(2,1)S(1)} %multiply_convert_fusion.9) | copy-start | bytes 786436
  259.2 290.4 %copy-start.7 = (bf16[2,64,2048]{2,1,0:T(8,128)(2,1)S(1)}, bf16[2,64,2048]{2,1,0:T(8,128)(2,1)}, u32[]{:S(2)}) copy-start(bf16[2,64,2048]{2,1,0:T(8,128)(2,1)} %param.21) | copy-start | bytes 1572868
  586.4 58.9 %copy-start.129 = (f32[64]{0:T(128)}, f32[64]{0:T(128)S(1)}, u32[]{:S(2)}) copy-start(f32[64]{0:T(128)S(1)} %broadcast_multiply_fusion.17) | copy-start | bytes 772
  655.9 743.7 %reduce-scatter.5.cloned.1.call-start = ((), (), s32[]{:S(2)}) async-start(), calls=%async_computation.8 | async-start | bytes 34078720 | tf_op jit(solution)/shard_map/reduce_scatter | solution.py:316
  657.2 14.3 copy-start.105
  711.6 1024.1 %reduce-scatter.11.cloned.1.call-start = ((), (), s32[]{:S(2)}) async-start(), calls=%async_computation.11 | async-start | bytes 51118080 | tf_op jit(solution)/shard_map/reduce_scatter | solution.py:328
  732.4 1561.9 %reduce-scatter.9.cloned.1.call-start = ((), (), s32[]{:S(2)}) async-start(), calls=%async_computation.10 | async-start | bytes 102236160 | tf_op jit(solution)/shard_map/reduce_scatter | solution.py:324
  770.3 1863.7 %all-reduce.14.cloned.1.call-start = ((), (), s32[]{:S(2)}) async-start(), calls=%async_computation.12 | async-start | bytes 3145728 | tf_op jit(solution)/shard_map/psum | solution.py:332
  771.9 11.2 copy-start.6
  771.9 11.2 copy-start.59
  771.9 11.2 copy-start.74
  783.2 12.2 copy-start.27
  783.2 12.2 copy-start.2
  795.4 13.7 copy-start.4
  820.7 1476.0 %copy-start.133 = (f32[128]{0:T(128)S(1)}, f32[128]{0:T(128)}, u32[]{:S(2)}) copy-start(f32[128]{0:T(128)} %get-tuple-element.12) | copy-start | bytes 1540
  820.7 1476.0 %copy-start.134 = (f32[128]{0:T(128)S(1)}, f32[128]{0:T(128)}, u32[]{:S(2)}) copy-start(f32[128]{0:T(128)} %get-tuple-element.102) | copy-start | bytes 1540
  820.7 1476.1 %copy-start.135 = (f32[128]{0:T(128)S(1)}, f32[128]{0:T(128)}, u32[]{:S(2)}) copy-start(f32[128]{0:T(128)} %get-tuple-element.26) | copy-start | bytes 1540
  820.7 1476.1 %copy-start.136 = (f32[128]{0:T(128)S(1)}, f32[128]{0:T(128)}, u32[]{:S(2)}) copy-start(f32[128]{0:T(128)} %get-tuple-element.24) | copy-start | bytes 1540
  820.7 1476.1 %copy-start.112 = (f32[2048]{0:T(1024)S(1)}, f32[2048]{0:T(1024)}, u32[]{:S(2)}) copy-start(f32[2048]{0:T(1024)} %get-tuple-element.16) | copy-start | bytes 24580
  820.7 1476.1 %copy-start.113 = (f32[2048]{0:T(1024)S(1)}, f32[2048]{0:T(1024)}, u32[]{:S(2)}) copy-start(f32[2048]{0:T(1024)} %get-tuple-element.14) | copy-start | bytes 24580
  820.7 1808.6 %copy-start.77 = (bf16[1,64,2048]{2,1,0:T(8,128)(2,1)S(1)}, bf16[1,64,2048]{2,1,0:T(8,128)(2,1)}, u32[]{:S(2)}) copy-start(bf16[1,64,2048]{2,1,0:T(8,128)(2,1)} %fusion.10) | copy-start | bytes 786436
  1401.4 1229.8 %copy-start.16 = (f32[64,2048]{1,0:T(8,128)S(1)}, f32[64,2048]{1,0:T(8,128)}, u32[]{:S(2)}) copy-start(f32[64,2048]{1,0:T(8,128)} %get-tuple-element.121) | copy-start | bytes 1572868
  1401.4 1229.8 %copy-start.90 = (f32[2048]{0:T(1024)S(1)}, f32[2048]{0:T(1024)}, u32[]{:S(2)}) copy-start(f32[2048]{0:T(1024)} %copy-done.89) | copy-start | bytes 24580
  1401.4 1229.8 %copy-start.126 = (f32[64]{0:T(128)S(1)}, f32[64]{0:T(128)}, u32[]{:S(2)}) copy-start(f32[64]{0:T(128)} %copy-done.125) | copy-start | bytes 772
  1401.4 1229.8 %copy-start.132 = (f32[64]{0:T(128)S(1)}, f32[64]{0:T(128)}, u32[]{:S(2)}) copy-start(f32[64]{0:T(128)} %copy-done.131) | copy-start | bytes 772
  2296.7 335.9 %copy-start.15 = (f32[64,2048]{1,0:T(8,128)S(1)}, f32[64,2048]{1,0:T(8,128)}, u32[]{:S(2)}) copy-start(f32[64,2048]{1,0:T(8,128)} %get-tuple-element.120) | copy-start | bytes 1572868
  2296.7 335.9 %copy-start.128 = (f32[64]{0:T(128)S(1)}, f32[64]{0:T(128)}, u32[]{:S(2)}) copy-start(f32[64]{0:T(128)} %copy-done.127) | copy-start | bytes 772
  2296.7 335.9 %copy-start.130 = (f32[64]{0:T(128)S(1)}, f32[64]{0:T(128)}, u32[]{:S(2)}) copy-start(f32[64]{0:T(128)} %copy-done.129) | copy-start | bytes 772
  (98 other events, 362.6 us)
Sparse Core Ops, SparseCore 0:
  11.2 110.3 all-gather.4
  124.8 81.4 all-gather.6
  209.5 207.8 all-gather.8
  420.4 129.0 all-gather.10
  656.1 358.0 reduce-scatter.6
  1016.4 383.1 reduce-scatter.4
  1406.0 329.5 reduce-scatter.10
  1742.1 552.1 reduce-scatter.8
  2298.1 56.2 all-reduce.13
where the time goes:
time: 2660 us; the launch traced here: 2650 us
  waiting for transfers between devices  1740 us (65%)
  blocking collectives  507 us (19%)
  matrix products  291 us (11%)
  other arithmetic  48.3 us (2%)
  local copies, waits for them, and re-layouts  42.7 us (2%)
    reduce_scatter x1, waiting for transfers between devices, on_device(): lax.psum_scatter(contract_first(columns_in, gate_up_all), 'fsdp', scatter...  557 us
    unnamed x2, blocking collectives  502 us
    reduce_scatter x1, waiting for transfers between devices, on_device(): lax.psum_scatter(qkv_term, 'fsdp', scatter_dimension=0, tiled=True)  384 us
    reduce_scatter x1, waiting for transfers between devices, on_device(): lax.psum_scatter(contract_first(columns_in, out_low_all), 'fsdp', scatter...  334 us
    reduce_scatter x1, waiting for transfers between devices, on_device(): lax.psum_scatter(out_term, 'fsdp', scatter_dimension=0, tiled=True)  193 us
    all_gather x1, waiting for transfers between devices, ffn_fetch(): lax.all_gather(ffn_weight, 'fsdp', axis=0, tiled=True)  158 us
    all_gather x1, waiting for transfers between devices, ffn_fetch(): lax.all_gather(down_weight, 'fsdp', axis=0, tiled=True)  110 us
    dot_general x8, matrix products, contract_last(): lax.dot_general(left_side, right_side, (((1,), (1,)), ((), ())), preferre...  109 us
  transfers between devices with their start and end apart: 9, of which 6 were waited for; matrix products, arithmetic and copies ran while one was open for 10% of the time, Pallas kernels for 0%

commit v1 on v0

v1 whole, which is shorter than its diff:
```python
import itertools

import jax
import jax.numpy as jnp
import numpy as np
from jax import lax
from jax.experimental import pallas as pl
from jax.experimental.pallas import tpu as pltpu
from jax.sharding import Mesh
from jax.sharding import PartitionSpec as P

D = 2048
H = 16
KVH = 8
HD = 128
FF = 6144
SEQ = 64
RANKS = 8
QCOLS = 2 * HD
CCOLS = 4 * HD
FCOLS = FF // RANKS
BLOCK = 256
SUB = 128

EPS = 1e-06
NEG = -1e30
BASE = 1000000.0
SCALE = HD**-0.5
BF = jnp.bfloat16
F32 = jnp.float32

AXES = ("zl", "y", "zh", "x", "c")
SIZES = {"zl": 2, "y": 4, "zh": 2, "x": 4, "c": 2}


def place(d):
    i = 0
    for a in AXES:
        i = i * SIZES[a] + d[a]
    return i


def pairs(move):
    found = []
    for t in itertools.product(*[range(SIZES[a]) for a in AXES]):
        d = dict(zip(AXES, t))
        e = move(dict(d))
        if e is not None:
            found.append((place(d), place(e)))
    return found


def step(axis, by):
    def move(d):
        if axis == "z":
            z = (d["zh"] * 2 + d["zl"] + by) % 4
            d["zh"], d["zl"] = z // 2, z % 2
        else:
            d[axis] = (d[axis] + by) % SIZES[axis]
        return d

    return move


def send(v, move):
    return lax.ppermute(v, AXES, pairs(move))


def partner(d):
    d["zl"], d["zh"] = 1 - d["zl"], 1 - d["zh"]
    return d


def spread_rows(half):
    def move(d):
        if d["y"] // 2 != d["zl"]:
            return None
        return {
            "zl": d["zl"],
            "y": d["x"],
            "zh": d["zh"],
            "x": 2 * d["c"] + half,
            "c": d["y"] % 2,
        }

    return move


def collect_rows(half):
    def move(d):
        if d["x"] % 2 != half:
            return None
        return {
            "zl": d["zl"],
            "y": 2 * d["zl"] + d["c"],
            "zh": d["zh"],
            "x": d["y"],
            "c": d["x"] // 2,
        }

    return move


def share_rows(d):
    if d["y"] // 2 != d["zl"]:
        return None
    d["zl"] = 1 - d["zl"]
    return d


def ring(v, axis):
    return [
        v,
        send(v, step(axis, -1)),
        send(v, step(axis, 2)),
        send(v, step(axis, 1)),
    ]


def gather_group(v):
    same = jnp.concatenate(ring(v, "z"), axis=0)
    return jnp.concatenate([same, send(same, step("c", 1))], axis=0)


def sum_group(parts, rows):
    half = 4 * rows
    other = send(parts[half:], step("c", 1))
    both = parts[:half].astype(F32) + other.astype(F32)
    low = both.astype(BF)
    one = send(low[rows : 2 * rows], step("z", 1))
    two = send(low[2 * rows : 3 * rows], step("z", 2))
    three = send(low[3 * rows :], step("z", -1))
    return (
        both[:rows] + one.astype(F32) + two.astype(F32) + three.astype(F32)
    )


def in_order(found, mine):
    twice = jnp.stack(found + found, axis=0)
    return lax.dynamic_slice_in_dim(twice, 4 - mine, 4, axis=0)


def last(a, b):
    return lax.dot_general(a, b, (((1,), (1,)), ((), ())), preferred_element_type=F32)


def first(a, b):
    return lax.dot_general(a, b, (((0,), (0,)), ((), ())), preferred_element_type=F32)


def plain(a, b):
    return jnp.dot(a, b, preferred_element_type=F32)


def root(v):
    return lax.rsqrt(jnp.mean(v * v, axis=-1, keepdims=True) + EPS)


def rotate(v, cos, sin):
    return v * cos + pltpu.roll(v, HD // 2, 1) * sin


def unrotate(v, cos, sin):
    return v * cos + pltpu.roll(v * sin, HD // 2, 1)


def scores_of(query, key, keep):
    s = last(query, key) * SCALE
    s = jnp.where(keep, s, NEG)
    p = jnp.exp(s - jnp.max(s, axis=-1, keepdims=True))
    return p / jnp.sum(p, axis=-1, keepdims=True)


def keep_mask(doc_col, doc_row):
    shape = (SUB, SUB)
    a = lax.broadcasted_iota(jnp.int32, shape, 0)
    b = lax.broadcasted_iota(jnp.int32, shape, 1)
    keep = (doc_col == doc_row) & (b <= a)
    return jnp.concatenate([keep, keep], axis=0)


def heads_of(qkv, gains, cos, sin):
    q0, q1, k = qkv[:, :HD], qkv[:, HD:QCOLS], qkv[:, QCOLS : QCOLS + HD]
    gq, gk = gains[0:1], gains[1:2]
    r0, r1, rk = root(q0), root(q1), root(k)
    z0, z1, zk = q0 * r0, q1 * r1, k * rk
    a0 = rotate(z0 * gq, cos, sin).astype(BF)
    a1 = rotate(z1 * gq, cos, sin).astype(BF)
    ak = rotate(zk * gk, cos, sin).astype(BF)
    val = qkv[:, QCOLS + HD :].astype(BF)
    return (r0, r1, rk), (z0, z1, zk), (a0, a1, ak), val


def attn_forward(x, w, wo, dcol, drow, cos, sin, gains, z_out, qkv_out, mix_out, part_out):
    xf = x[...].astype(F32)
    z = (xf * root(xf)).astype(BF)
    z_out[...] = z
    qkv = plain(z, w[...])
    qkv_out[...] = qkv
    _, _, (a0, a1, ak), val = heads_of(qkv, gains[...], cos[...], sin[...])
    for s in range(BLOCK // SUB):
        r = slice(s * SUB, (s + 1) * SUB)
        keep = keep_mask(dcol[r, :], drow[0, :, r])
        p = scores_of(jnp.concatenate([a0[r], a1[r]], axis=0), ak[r], keep)
        o = plain(p.astype(BF), val[r])
        mix_out[r, :HD] = o[:SUB].astype(BF)
        mix_out[r, HD:] = o[SUB:].astype(BF)
    part_out[...] = plain(mix_out[...], wo[...]).astype(BF)


def norm_back(r, z, gain, e):
    eg = e * gain
    return r * (eg - z * jnp.mean(eg * z, axis=-1, keepdims=True)), jnp.sum(
        e * z, axis=0, keepdims=True
    )


def attn_backward(g, qkv_in, w, wo, dcol, drow, cos, sin, gains, gqkv_out, part_out, gain_out):
    gm = last(g[...], wo[...]).astype(BF)
    gain = gains[...]
    c, s_ = cos[...], sin[...]
    (r0, r1, rk), (z0, z1, zk), (a0, a1, ak), val = heads_of(qkv_in[...], gain, c, s_)
    d0, d1, dk, dv = [], [], [], []
    for s in range(BLOCK // SUB):
        r = slice(s * SUB, (s + 1) * SUB)
        keep = keep_mask(dcol[r, :], drow[0, :, r])
        q = jnp.concatenate([a0[r], a1[r]], axis=0)
        do = jnp.concatenate([gm[r, :HD], gm[r, HD:]], axis=0)
        p = scores_of(q, ak[r], keep)
        dp = last(do, val[r])
        ds = (p * (dp - jnp.sum(p * dp, axis=-1, keepdims=True))).astype(BF)
        dq = plain(ds, ak[r]) * SCALE
        d0.append(dq[:SUB])
        d1.append(dq[SUB:])
        dk.append(first(ds, q) * SCALE)
        dv.append(first(p.astype(BF), do))
    d0, d1, dk, dv = [jnp.concatenate(v, axis=0) for v in (d0, d1, dk, dv)]
    g0, t0 = norm_back(r0, z0, gain[0:1], unrotate(d0, c, s_))
    g1, t1 = norm_back(r1, z1, gain[0:1], unrotate(d1, c, s_))
    gk, tk = norm_back(rk, zk, gain[1:2], unrotate(dk, c, s_))
    gqkv_out[:, :HD] = g0.astype(BF)
    gqkv_out[:, HD:QCOLS] = g1.astype(BF)
    gqkv_out[:, QCOLS : QCOLS + HD] = gk.astype(BF)
    gqkv_out[:, QCOLS + HD :] = dv.astype(BF)
    part_out[...] = last(gqkv_out[...], w[...]).astype(BF)

    @pl.when(pl.program_id(0) == 0)
    def _():
        gain_out[...] = jnp.zeros_like(gain_out)

    gain_out[0:1] += t0 + t1
    gain_out[1:2] += tk


def whole(*shape):
    return pl.BlockSpec(shape, lambda i: (0,) * len(shape))


def rows_of(width):
    return pl.BlockSpec((BLOCK, width), lambda i: (i, 0))


PARAMS = pltpu.CompilerParams(
    dimension_semantics=("arbitrary",), vmem_limit_bytes=48 * 1024 * 1024
)


def call_forward(x, w, wo, dcol, drow, cos, sin, gains):
    n = x.shape[0]
    return pl.pallas_call(
        attn_forward,
        grid=(n // BLOCK,),
        in_specs=[
            rows_of(D),
            whole(D, CCOLS),
            whole(QCOLS, D),
            rows_of(1),
            pl.BlockSpec((1, 1, BLOCK), lambda i: (i, 0, 0)),
            whole(BLOCK, HD),
            whole(BLOCK, HD),
            whole(8, HD),
        ],
        out_specs=[rows_of(D), rows_of(CCOLS), rows_of(QCOLS), rows_of(D)],
        out_shape=[
            jax.ShapeDtypeStruct((n, D), BF),
            jax.ShapeDtypeStruct((n, CCOLS), F32),
            jax.ShapeDtypeStruct((n, QCOLS), BF),
            jax.ShapeDtypeStruct((n, D), BF),
        ],
        compiler_params=PARAMS,
        cost_estimate=pl.CostEstimate(
            flops=2 * n * D * (CCOLS + QCOLS), bytes_accessed=16 << 20, transcendentals=n * 256
        ),
    )(x, w, wo, dcol, drow, cos, sin, gains)


def call_backward(g, qkv, w, wo, dcol, drow, cos, sin, gains):
    n = g.shape[0]
    return pl.pallas_call(
        attn_backward,
        grid=(n // BLOCK,),
        in_specs=[
            rows_of(D),
            rows_of(CCOLS),
            whole(D, CCOLS),
            whole(QCOLS, D),
            rows_of(1),
            pl.BlockSpec((1, 1, BLOCK), lambda i: (i, 0, 0)),
            whole(BLOCK, HD),
            whole(BLOCK, HD),
            whole(8, HD),
        ],
        out_specs=[rows_of(CCOLS), rows_of(D), whole(8, HD)],
        out_shape=[
            jax.ShapeDtypeStruct((n, CCOLS), BF),
            jax.ShapeDtypeStruct((n, D), BF),
            jax.ShapeDtypeStruct((8, HD), F32),
        ],
        compiler_params=PARAMS,
        cost_estimate=pl.CostEstimate(
            flops=2 * n * D * (CCOLS + QCOLS), bytes_accessed=16 << 20, transcendentals=n * 256
        ),
    )(g, qkv, w, wo, dcol, drow, cos, sin, gains)


def tables():
    half = HD // 2
    freq = BASE ** (-(np.arange(half, dtype=np.float64) * 2.0 / HD))
    angles = np.arange(SEQ, dtype=np.float64)[:, None] * freq
    cos = np.concatenate([np.cos(angles)] * 2, axis=-1)
    sin = np.concatenate([-np.sin(angles), np.sin(angles)], axis=-1)
    reps = (BLOCK // SEQ, 1)
    return np.tile(cos, reps).astype(np.float32), np.tile(sin, reps).astype(np.float32)


def rank_pieces(shard, cuts):
    made = []
    for zl, zh, c in itertools.product(range(2), range(2), range(2)):
        t = 4 * zl + 2 * c + zh
        made.append(
            jnp.concatenate(
                [shard[:, at + t * width : at + (t + 1) * width] for at, width in cuts],
                axis=1,
            )
        )
    return jnp.stack(made).reshape((2, 2, 2) + made[0].shape)


def pick(v, *at):
    for i in at:
        v = lax.dynamic_index_in_dim(v, i, 0, keepdims=False)
    return v


def my_columns(shard, cuts, zl, zh, c):
    pieces = rank_pieces(shard, cuts)
    near, far = pick(pieces, zl, zh), pick(pieces, 1 - zl, 1 - zh)
    keep = jnp.stack([pick(near, c), pick(far, c)])
    give = jnp.stack([pick(near, 1 - c), pick(far, 1 - c)])
    got = send(give, step("c", 1))
    by_c = jnp.where(
        c == 0, jnp.stack([keep, got], axis=1), jnp.stack([got, keep], axis=1)
    )
    beyond = send(by_c[1], partner)
    mine = by_c[0]
    return jnp.where(
        zh == 0, jnp.stack([mine, beyond]), jnp.stack([beyond, mine])
    )


def own_rows(part, cuts, columns, zl, zh, c):
    z = 2 * zh + zl

    def to(by):
        return pick(part, ((z + by) % 4) // 2)

    found = [
        to(0),
        send(to(-1), step("z", -1)),
        send(to(2), step("z", 2)),
        send(to(1), step("z", 1)),
    ]
    by_z = in_order(found, z)
    by_z = by_z.reshape((2, 2) + by_z.shape[1:])
    keep = lax.dynamic_index_in_dim(by_z, c, 2, keepdims=False)
    give = lax.dynamic_index_in_dim(by_z, 1 - c, 2, keepdims=False)
    got = send(give, step("c", 1))
    low = jnp.where(c == 0, keep, got)
    high = jnp.where(c == 0, got, keep)
    made = []
    at = 0
    for _, width in cuts:
        for zl_, c_, zh_ in itertools.product(range(2), range(2), range(2)):
            made.append((low if c_ == 0 else high)[zh_, zl_, :, at : at + width])
        at += width
    return jnp.concatenate(made, axis=1).astype(F32)


QKV_CUTS = ((0, QCOLS), (H * HD, HD), ((H + KVH) * HD, HD))
FFN_CUTS = ((0, FCOLS), (FF, FCOLS))
WIDE = 512


def fold(v):
    return jnp.concatenate(
        [v[:, i : i + WIDE] for i in range(0, v.shape[1], WIDE)], axis=0
    )


def to_plane(u):
    return u.reshape(4, 2, 4, 64, u.shape[-1]).transpose(0, 2, 1, 3, 4)


def layer(
    tokens,
    segments,
    qkv_weight,
    out_weight,
    attn_gain,
    query_gain,
    key_gain,
    ffn_weight,
    down_weight,
    ffn_gain,
    out_grad,
):
    zl, y, zh, x, c = [lax.axis_index(a) for a in AXES]
    z = 2 * zh + zl
    seqs = tokens.shape[0]
    rows = seqs * SEQ
    x_own = tokens.reshape(rows, D)
    g_own = out_grad.reshape(rows, D)

    gain_in = attn_gain.astype(F32)[:, None]
    gain_mid = ffn_gain.astype(F32)[:, None]
    qkv_mine = my_columns(
        (qkv_weight.astype(F32) * gain_in).astype(BF), QKV_CUTS, zl, zh, c
    ).reshape(128, CCOLS)
    halves = jnp.concatenate(
        [out_weight.reshape(2, 16, D), down_weight.reshape(2, 48, D)], axis=1
    )
    rows_mine = send(halves[0], spread_rows(0)) + send(halves[1], spread_rows(1))
    attn_pack = jnp.concatenate([qkv_mine, fold(rows_mine[:16])], axis=0)
    attn_all = lax.all_gather(attn_pack, ("y", "x"), axis=0, tiled=False)
    ffn_mine = my_columns(
        (ffn_weight.astype(F32) * gain_mid).astype(BF), FFN_CUTS, zl, zh, c
    ).reshape(128, 2 * FCOLS)
    ffn_pack = jnp.concatenate([fold(ffn_mine), fold(rows_mine[16:])], axis=0)
    ffn_all = lax.all_gather(ffn_pack, ("y", "x"), axis=0, tiled=False)

    w_qkv = (
        attn_all[:, :128]
        .reshape(4, 4, 2, 64, WIDE)
        .transpose(0, 2, 1, 3, 4)
        .reshape(D, CCOLS)
    )
    w_out = (
        attn_all[:, 128:].reshape(16, 4, 16, WIDE).transpose(0, 2, 1, 3).reshape(QCOLS, D)
    )
    w_ffn = (
        ffn_all[:, :384]
        .reshape(4, 4, 3, 2, 64, WIDE)
        .transpose(0, 3, 1, 4, 2, 5)
        .reshape(D, 2 * FCOLS)
    )
    w_down = (
        ffn_all[:, 384:].reshape(16, 4, 48, WIDE).transpose(0, 2, 1, 3).reshape(FCOLS, D)
    )

    f = ((y * 2 + zh) * 4 + x) * 2 + c
    spots = jnp.stack([query_gain, key_gain]).astype(F32)
    mine = lax.dynamic_update_slice(jnp.zeros((2, HD), F32), spots, (0, 2 * f))
    note = jnp.concatenate([segments.reshape(1, rows).astype(F32), mine], axis=0)
    note = jnp.stack(ring(note, "z"))
    note = jnp.concatenate([note, send(note, step("c", 1))], axis=0)
    docs = note[:, 0].reshape(-1)
    near = jnp.where(zl == 0, note[3] + note[7], note[1] + note[5])
    gains = (note[0] + note[4] + near)[1:]
    gains = sum(ring(gains, "x"))
    gains = sum(ring(gains, "y"))
    gains = jnp.pad(gains, ((0, 6), (0, 0)))
    total = docs.shape[0]
    docs = docs + 8.0 * (jnp.arange(total) // SEQ).astype(F32)
    dcol = docs.reshape(total, 1)
    drow = docs.reshape(total // BLOCK, 1, BLOCK)
    cos, sin = tables()

    x_all = gather_group(x_own)
    z_in, qkv, mixed, part = call_forward(x_all, w_qkv, w_out, dcol, drow, cos, sin, gains)
    hidden = x_own.astype(F32) + sum_group(part, rows)
    r_mid = root(hidden)
    z_mid_own = hidden * r_mid
    z_mid = gather_group(z_mid_own.astype(BF))
    g_all = gather_group(g_own)
    gate_up = plain(z_mid, w_ffn)
    gate, up = gate_up[:, :FCOLS], gate_up[:, FCOLS:]
    g_active = last(g_all, w_down)
    sig = jax.nn.sigmoid(gate)
    active = (gate * sig * up).astype(BF)
    g_gate = (g_active * up * sig * (1.0 + gate * (1.0 - sig))).astype(BF)
    g_up = (g_active * gate * sig).astype(BF)
    g_gate_up = jnp.concatenate([g_gate, g_up], axis=1)

    eg = sum_group(last(g_gate_up, w_ffn).astype(BF), rows)
    g_hidden = g_own.astype(F32) + r_mid * (
        eg - z_mid_own * jnp.mean(eg * z_mid_own, axis=-1, keepdims=True)
    )
    result = hidden + sum_group(plain(active, w_down).astype(BF), rows)

    u_ffn = first(z_mid, g_gate_up).astype(BF)
    u_down = first(active, g_all).astype(BF)
    ffn_sum = jnp.concatenate(
        [
            to_plane(u_ffn)
            .reshape(16, 128, 3, WIDE)
            .transpose(0, 2, 1, 3)
            .reshape(16, 384, WIDE),
            u_down.reshape(16, 48, 4, WIDE).transpose(0, 2, 1, 3).reshape(16, 192, WIDE),
        ],
        axis=1,
    )
    ffn_sum = lax.psum_scatter(
        ffn_sum.reshape(16 * 576, WIDE), ("y", "x"), scatter_dimension=0, tiled=True
    )

    g_low = gather_group(g_hidden.astype(BF))
    g_qkv, part, gain_part = call_backward(
        g_low, qkv, w_qkv, w_out, dcol, drow, cos, sin, gains
    )
    eg = sum_group(part, rows)
    x_f32 = x_own.astype(F32)
    r_in = root(x_f32)
    z_own = x_f32 * r_in
    g_tokens = g_hidden + r_in * (
        eg - z_own * jnp.mean(eg * z_own, axis=-1, keepdims=True)
    )

    u_qkv = first(z_in, g_qkv).astype(BF)
    u_out = first(mixed, g_low).astype(BF)
    attn_sum = jnp.concatenate(
        [
            to_plane(u_qkv).reshape(16, 128, WIDE),
            u_out.reshape(16, 16, 4, WIDE).transpose(0, 2, 1, 3).reshape(16, 64, WIDE),
        ],
        axis=1,
    )
    attn_sum = lax.psum_scatter(
        attn_sum.reshape(16 * 192, WIDE), ("y", "x"), scatter_dimension=0, tiled=True
    )

    u_qkv = own_rows(attn_sum[:128].reshape(2, 2, 32, CCOLS), QKV_CUTS, 4096, zl, zh, c)
    u_ffn = own_rows(
        ffn_sum[:384]
        .reshape(3, 128, WIDE)
        .transpose(1, 0, 2)
        .reshape(2, 2, 32, 2 * FCOLS),
        FFN_CUTS,
        2 * FF,
        zl,
        zh,
        c,
    )
    rows_sum = jnp.concatenate(
        [
            attn_sum[128:].reshape(4, 16, WIDE).transpose(1, 0, 2).reshape(16, D),
            ffn_sum[384:].reshape(4, 48, WIDE).transpose(1, 0, 2).reshape(48, D),
        ],
        axis=0,
    )
    halves = jnp.stack(
        [send(rows_sum, collect_rows(0)), send(rows_sum, collect_rows(1))]
    )
    halves = halves + send(halves, share_rows)
    d_out = halves[:, :16].reshape(32, D).astype(F32)
    d_down = halves[:, 16:].reshape(96, D).astype(F32)

    gain_sum = gain_part[:2]
    for axis in ("c", "z", "x", "y"):
        if axis == "c":
            gain_sum = gain_sum + send(gain_sum, step("c", 1))
        else:
            gain_sum = sum(ring(gain_sum, axis))
    gain_own = lax.dynamic_slice(gain_sum, (0, 2 * f), (2, 2))

    return (
        result.astype(BF).reshape(seqs, SEQ, D),
        g_tokens.reshape(seqs, SEQ, D),
        u_qkv * gain_in,
        d_out,
        jnp.sum(u_qkv * qkv_weight.astype(F32), axis=1),
        gain_own[0],
        gain_own[1],
        u_ffn * gain_mid,
        d_down,
        jnp.sum(u_ffn * ffn_weight.astype(F32), axis=1),
    )


def solution(mesh):
    fine = Mesh(mesh.devices.reshape([SIZES[a] for a in AXES]), AXES)
    batch = AXES
    shard = ("y", "zh", "x", "c")
    matrix = P(shard, None)
    vector = P(shard)
    return jax.shard_map(
        layer,
        mesh=fine,
        in_specs=(
            P(batch, None, None),
            P(batch, None),
            matrix,
            matrix,
            vector,
            vector,
            vector,
            matrix,
            matrix,
            vector,
            P(batch, None, None),
        ),
        out_specs=(
            P(batch, None, None),
            P(batch, None, None),
            matrix,
            matrix,
            vector,
            vector,
            vector,
            matrix,
            matrix,
            vector,
        ),
        check_vma=False,
    )
```

time: 2660 us -> 604 us (0.23)
  waiting for transfers between devices: 1740 us -> 250 us
  blocking collectives: 507 us -> 0 us
  matrix products: 291 us -> 48.8 us
  starting transfers between devices: 0.97 us -> 102 us
  local copies, waits for them, and re-layouts: 42.7 us -> 114 us
    reduce_scatter x4 -> x2, waiting for transfers between devices: 1470 us -> 37.6 us  [the longest x1 37.6 us: layer(): lax.psum_scatter(ffn_sum.reshape(16 * 576, WIDE), ('y', 'x'), scatter_dim...]
    unnamed x2 -> x0, blocking collectives: 502 us -> none
    all_gather x4 -> x2, waiting for transfers between devices: 269 us -> 0.01 us  [the longest x1 0.01 us: layer(): attn_all = lax.all_gather(attn_pack, ('y', 'x'), axis=0, tiled=False)]
    dot_general x32 -> x8, matrix products: 291 us -> 48.8 us  [the longest x4 21.4 us: first(): lax.dot_general(a, b, (((0,), (0,)), ((), ())), preferred_element_type=F32)]
    ppermute x0 -> x69, waiting for transfers between devices: none -> 213 us  [send(): return lax.ppermute(v, AXES, pairs(move))]
    ppermute x0 -> x69, starting transfers between devices: none -> 101 us  [send(): return lax.ppermute(v, AXES, pairs(move))]
    reshape x9 -> x11, local copies, waits for them, and re-layouts: 9.65 us -> 37.8 us  [the longest x1 18.7 us: layer(): ffn_sum = jnp.concatenate([to_plane(u_ffn).reshape(16, 128, 3, WIDE).tran...]
  transfers between devices with their start and end apart: 9 -> 73, of which waited for: 6 -> 41; matrix products, arithmetic and copies ran while one was open for 10% -> 19% of each run, Pallas kernels for 0% -> 2%
where the time goes in v1:
time: 604 us; the launch traced here: 592 us
  waiting for transfers between devices  250 us (41%)
  local copies, waits for them, and re-layouts  114 us (19%)
  starting transfers between devices  102 us (17%)
  matrix products  48.8 us (8%)
  other arithmetic  34.9 us (6%)
  Pallas kernels  26.1 us (4%)
  between operations  16.1 us (3%)
    ppermute x69, waiting for transfers between devices, send(): return lax.ppermute(v, AXES, pairs(move))  213 us
    ppermute x69, starting transfers between devices, send(): return lax.ppermute(v, AXES, pairs(move))  101 us
    reduce_scatter x1, waiting for transfers between devices, layer(): lax.psum_scatter(ffn_sum.reshape(16 * 576, WIDE), ('y', 'x'), scatter_dim...  37.6 us
    unnamed x153, local copies, waits for them, and re-layouts  25.6 us
    dot_general x4, matrix products, first(): lax.dot_general(a, b, (((0,), (0,)), ((), ())), preferred_element_type=F32)  21.4 us
    reshape x1, local copies, waits for them, and re-layouts, layer(): ffn_sum = jnp.concatenate([to_plane(u_ffn).reshape(16, 128, 3, WIDE).tran...  18.7 us
    pallas_call x1, Pallas kernels, call_backward(): pl.pallas_call(attn_backward, grid=(n // BLOCK,), in_specs=[rows_of(D), r...  14.7 us
    dot_general x2, matrix products, plain(): return jnp.dot(a, b, preferred_element_type=F32)  13.9 us
  transfers between devices with their start and end apart: 73, of which 41 were waited for; matrix products, arithmetic and copies ran while one was open for 19% of the time, Pallas kernels for 2%

profile of v1, /device:TPU:0, one launch (start us, length us, event | category | flops | bytes accessed | tf_op | source)
XLA Modules:
  0.0 591.9 jit_solution(6684555917430405409)
XLA Ops:
  10.7 4.2 collective-permute-start.5
  16.0 3.4 collective-permute-start.7
  24.7 6.3 %collective-permute-start.26 = (bf16[2,32,1536]{2,1,0:T(8,128)(2,1)S(1)}, bf16[2,32,1536]{2,1,0:T(8,128)(2,1)S(1)}, u32[]{:S(2)}, u32[]{:S(2)}) collective-permute-start(bf16[2,32,1536]{2,1,0:T(8,128)(2,1)S(1)} %pad_maximum_fusion.11), channel_id=1, source_target_pairs={{0,1},{1,0},{2,3},{3,2},{4,5},{5,4},{6,7},{7,6},{8,9},{9,8},{10,11... | collective-permute-start | bytes 589832 | tf_op jit(solution)/shard_map/ppermute | solution.py:66
  33.5 7.1 %collective-permute-done.27 = bf16[2,32,1536]{2,1,0:T(8,128)(2,1)S(1)} collective-permute-done((bf16[2,32,1536]{2,1,0:T(8,128)(2,1)S(1)}, bf16[2,32,1536]{2,1,0:T(8,128)(2,1)S(1)}, u32[]{:S(2)}, u32[]{:S(2)}) %collective-permute-start.27) | collective-permute-done | bytes 196640 | tf_op jit(solution)/shard_map/ppermute | solution.py:66
  51.5 8.0 %collective-permute-done.2 = bf16[128,2048]{1,0:T(8,128)(2,1)S(1)} collective-permute-done((bf16[128,2048]{1,0:T(8,128)(2,1)S(1)}, bf16[128,2048]{1,0:T(8,128)(2,1)S(1)}, u32[]{:S(2)}, u32[]{:S(2)}) %collective-permute-start.2) | collective-permute-done | bytes 524320 | tf_op jit(solution)/shard_map/ppermute | solution.py:66
  59.5 11.3 %collective-permute-done.1 = bf16[128,2048]{1,0:T(8,128)(2,1)S(1)} collective-permute-done((bf16[128,2048]{1,0:T(8,128)(2,1)S(1)}, bf16[128,2048]{1,0:T(8,128)(2,1)S(1)}, u32[]{:S(2)}, u32[]{:S(2)}) %collective-permute-start.1) | collective-permute-done | bytes 524320 | tf_op jit(solution)/shard_map/ppermute | solution.py:66
  72.4 4.7 collective-permute-start.13
  101.4 11.4 %shard_map.204 = (bf16[1024,2048]{1,0:T(8,128)(2,1)}, f32[1024,512]{1,0:T(8,128)S(1)}, bf16[1024,256]{1,0:T(8,128)(2,1)S(1)}, bf16[1024,2048]{1,0:T(8,128)(2,1)}) custom-call(bf16[1024,2048]{1,0:T(8,128)(2,1)} %constant_dynamic-update-slice_fusion.x, bf16[2048,512]{1,0:T(8,128)(2,1)} %bitcast.471, bf16[256,2048]{1,0:T(8,128)(2,1)S(1)} %bitcast.432, ...), custom_call_target="tpu_custom_call" | custom-call | flops 3221225472 | bytes 16777216 | tf_op jit(solution)/shard_map/pallas_call | solution.py:270
  128.0 3.9 collective-permute-done.34
  134.2 10.0 %collective-permute-done.33 = bf16[128,2048]{1,0:T(8,128)(2,1)S(1)} collective-permute-done((bf16[128,2048]{1,0:T(8,128)(2,1)S(1)}, bf16[128,2048]{1,0:T(8,128)(2,1)S(1)}, u32[]{:S(2)}, u32[]{:S(2)}) %collective-permute-start.33) | collective-permute-done | bytes 524320 | tf_op jit(solution)/shard_map/ppermute | solution.py:66
  144.5 9.4 %collective-permute-done.19 = bf16[128,2048]{1,0:T(8,128)(2,1)S(1)} collective-permute-done((bf16[128,2048]{1,0:T(8,128)(2,1)S(1)}, bf16[128,2048]{1,0:T(8,128)(2,1)S(1)}, u32[]{:S(2)}, u32[]{:S(2)}) %collective-permute-start.19) | collective-permute-done | bytes 524320 | tf_op jit(solution)/shard_map/ppermute | solution.py:66
  155.3 10.9 %collective-permute-done.20 = bf16[128,2048]{1,0:T(8,128)(2,1)S(1)} collective-permute-done((bf16[128,2048]{1,0:T(8,128)(2,1)S(1)}, bf16[128,2048]{1,0:T(8,128)(2,1)S(1)}, u32[]{:S(2)}, u32[]{:S(2)}) %collective-permute-start.20) | collective-permute-done | bytes 524320 | tf_op jit(solution)/shard_map/ppermute | solution.py:66
  173.4 11.3 %collective-permute-done.24 = bf16[128,2048]{1,0:T(8,128)(2,1)S(1)} collective-permute-done((bf16[128,2048]{1,0:T(8,128)(2,1)S(1)}, bf16[128,2048]{1,0:T(8,128)(2,1)S(1)}, u32[]{:S(2)}, u32[]{:S(2)}) %collective-permute-start.24) | collective-permute-done | bytes 524320 | tf_op jit(solution)/shard_map/ppermute | solution.py:66
  184.8 9.9 %collective-permute-done.23 = bf16[128,2048]{1,0:T(8,128)(2,1)S(1)} collective-permute-done((bf16[128,2048]{1,0:T(8,128)(2,1)S(1)}, bf16[128,2048]{1,0:T(8,128)(2,1)S(1)}, u32[]{:S(2)}, u32[]{:S(2)}) %collective-permute-start.23) | collective-permute-done | bytes 524320 | tf_op jit(solution)/shard_map/ppermute | solution.py:66
  203.4 6.0 %slice.641 = bf16[16,384,512]{2,1,0:T(8,128)(2,1)} slice(bf16[16,576,512]{2,1,0:T(8,128)(2,1)} %bitcast.450), slice={[0:16], [0:384], [0:512]} | slice | bytes 12582912 | tf_op jit(solution)/shard_map/slice | solution.py:461
  214.7 12.1 %copy.61 = bf16[4,2,4,64,3,512]{5,4,3,2,1,0:T(4,128)(2,1)} copy(bf16[4,2,4,64,3,512]{5,3,1,4,2,0:T(8,128)(2,1)} %bitcast.438) | data formatting | bytes 12582912 | tf_op jit(solution)/shard_map/transpose | solution.py:463
  226.8 6.5 %copy.77 = bf16[256,8,3,512]{3,1,2,0:T(8,128)(2,1)S(1)} copy(bf16[256,8,3,512]{3,2,1,0:T(4,128)(2,1)} %bitcast.435) | data formatting | bytes 12582912
  233.3 10.2 %fusion.48 = f32[1024,1536]{1,0:T(8,128)} fusion(bf16[1024,2048]{1,0:T(8,128)(2,1)} %constant_dynamic-update-slice_fusion.23, bf16[2048,1536]{1,0:T(8,128)(2,1)S(1)} %bitcast.453), kind=kOutput, calls=%fused_computation.322 | convolution fusion | flops 6442450944 | bytes 16777216 | tf_op jit(solution)/shard_map/dot_general | solution.py:152
  243.6 6.6 %multiply_convert_fusion.1 = (bf16[1024,768]{1,0:T(8,128)(2,1)S(1)}, bf16[1024,768]{1,0:T(8,128)(2,1)S(1)}, bf16[1024,768]{1,0:T(8,128)(2,1)S(1)}) fusion(f32[1024,1536]{1,0:T(8,128)} %fusion.48, bf16[1024,2048]{1,0:T(8,128)(2,1)S(1)} %copy-done.20, bf16[768,2048]{1,0:T(8,128)(2,1)S(1)} %bitcast.464), kind=kOutput, calls=%fused_computation.13 | convolution fusion | flops 3233808384 | bytes 18350080 | tf_op jit(solution)/shard_map/dot_general | solution.py:144
  251.3 6.9 %convolution_convert_fusion.1 = bf16[1024,2048]{1,0:T(8,128)(2,1)S(1)} fusion(bf16[2048,1536]{1,0:T(8,128)(2,1)S(1)} %bitcast.454, bf16[1024,768]{1,0:T(8,128)(2,1)S(1)} %get-tuple-element.31, bf16[1024,768]{1,0:T(8,128)(2,1)S(1)} %get-tuple-element.30), kind=kOutput, calls=%fused_computation.7 | convolution fusion | flops 6450839552 | bytes 13631488 | tf_op jit(solution)/shard_map/dot_general | solution.py:144
  258.6 3.6 convolution_convert_fusion.2
  273.0 7.9 %collective-permute-done.37 = bf16[128,2048]{1,0:T(8,128)(2,1)S(1)} collective-permute-done((bf16[128,2048]{1,0:T(8,128)(2,1)S(1)}, bf16[128,2048]{1,0:T(8,128)(2,1)S(1)}, u32[]{:S(2)}, u32[]{:S(2)}) %collective-permute-start.37) | collective-permute-done | bytes 524320 | tf_op jit(solution)/shard_map/ppermute | solution.py:66
  281.9 8.8 %collective-permute-done.39 = bf16[128,2048]{1,0:T(8,128)(2,1)S(1)} collective-permute-done((bf16[128,2048]{1,0:T(8,128)(2,1)S(1)}, bf16[128,2048]{1,0:T(8,128)(2,1)S(1)}, u32[]{:S(2)}, u32[]{:S(2)}) %collective-permute-start.39) | collective-permute-done | bytes 524320 | tf_op jit(solution)/shard_map/ppermute | solution.py:66
  292.6 9.1 %collective-permute-done.29 = bf16[128,2048]{1,0:T(8,128)(2,1)S(1)} collective-permute-done((bf16[128,2048]{1,0:T(8,128)(2,1)S(1)}, bf16[128,2048]{1,0:T(8,128)(2,1)S(1)}, u32[]{:S(2)}, u32[]{:S(2)}) %collective-permute-start.29) | collective-permute-done | bytes 524320 | tf_op jit(solution)/shard_map/ppermute | solution.py:66
  303.0 10.9 %collective-permute-done.30 = bf16[128,2048]{1,0:T(8,128)(2,1)S(1)} collective-permute-done((bf16[128,2048]{1,0:T(8,128)(2,1)S(1)}, bf16[128,2048]{1,0:T(8,128)(2,1)S(1)}, u32[]{:S(2)}, u32[]{:S(2)}) %collective-permute-start.30) | collective-permute-done | bytes 524320 | tf_op jit(solution)/shard_map/ppermute | solution.py:66
  320.8 21.7 %collective-permute-done.42 = bf16[128,2048]{1,0:T(8,128)(2,1)S(1)} collective-permute-done((bf16[128,2048]{1,0:T(8,128)(2,1)S(1)}, bf16[128,2048]{1,0:T(8,128)(2,1)S(1)}, u32[]{:S(2)}, u32[]{:S(2)}) %collective-permute-start.42) | collective-permute-done | bytes 524320 | tf_op jit(solution)/shard_map/ppermute | solution.py:66
  343.5 4.0 collective-permute-done.43
  349.8 14.7 %shard_map.205 = (bf16[1024,512]{1,0:T(8,128)(2,1)S(1)}, bf16[1024,2048]{1,0:T(8,128)(2,1)}, f32[8,128]{1,0:T(8,128)S(1)}) custom-call(bf16[1024,2048]{1,0:T(8,128)(2,1)} %copy-done.22, f32[1024,512]{1,0:T(8,128)S(1)} %copy-done.3, bf16[2048,512]{1,0:T(8,128)(2,1)} %bitcast.472, bf16[256,2048]{1,0:T(8,128)(2,1)S(1)} %bitcast.433, f32[1024,1]{1,0:T(8,128)S(1)} %add.394.dcol, ...), custom_call_target="tpu_custom_call" | custom-call | flops 3221225472 | bytes 16777216 | tf_op jit(solution)/shard_map/pallas_call | solution.py:299
  364.5 4.6 convolution_convert_fusion.5
  375.1 3.7 pad_maximum_fusion.2
  379.0 9.5 %convolution_convert_fusion = bf16[2048,1536]{1,0:T(8,128)(2,1)S(1)} fusion(bf16[1024,2048]{1,0:T(8,128)(2,1)} %constant_dynamic-update-slice_fusion.23, bf16[1024,768]{1,0:T(8,128)(2,1)} %copy-done.35, bf16[1024,768]{1,0:T(8,128)(2,1)S(1)} %copy-done.34), kind=kOutput, calls=%fused_computation.1 | convolution fusion | flops 6451888128 | bytes 13631488 | tf_op jit(solution)/shard_map/dot_general | solution.py:148
  388.6 3.9 copy.81
  393.6 4.9 convolution_convert_fusion.3
  398.5 6.2 %reshape.369 = bf16[16,48,4,512]{3,2,1,0:T(4,128)(2,1)} reshape(bf16[768,2048]{1,0:T(8,128)(2,1)} %convolution_convert_fusion.3) | data formatting | bytes 6291456 | tf_op jit(solution)/shard_map/reshape | solution.py:518
  404.7 4.5 copy.70
  409.1 18.7 %reshape.367 = bf16[16,128,3,512]{3,2,1,0:T(4,128)(2,1)} reshape(bf16[4,4,2,64,1536]{4,3,2,1,0:T(8,128)(2,1)} %bitcast.437) | data formatting | bytes 12582912 | tf_op jit(solution)/shard_map/reshape | solution.py:515
  427.8 5.5 copy.69
  433.4 4.0 pad_maximum_fusion
  441.3 3.4 collective-permute-done.55
  445.3 3.4 collective-permute-start.57
  464.7 3.5 convert_add_fusion
  472.4 18.9 %collective-permute-done.45 = bf16[128,2048]{1,0:T(8,128)(2,1)S(1)} collective-permute-done((bf16[128,2048]{1,0:T(8,128)(2,1)S(1)}, bf16[128,2048]{1,0:T(8,128)(2,1)S(1)}, u32[]{:S(2)}, u32[]{:S(2)}) %collective-permute-start.45) | collective-permute-done | bytes 524320 | tf_op jit(solution)/shard_map/ppermute | solution.py:66
  492.8 3.2 collective-permute-start.48
  500.4 4.5 collective-permute-done.49
  507.0 37.6 %reduce-scatter.5.cloned.1.call-done = bf16[576,512]{1,0:T(8,128)(2,1)} async-done(((bf16[9216,512]{1,0:T(8,128)(2,1)}), bf16[576,512]{1,0:T(8,128)(2,1)}) %reduce-scatter.5.cloned.1.call-update) | async-done | bytes 589840 | tf_op jit(solution)/shard_map/reduce_scatter | solution.py:522
  555.3 3.3 collective-permute-start.66
  558.6 9.1 %collective-permute-done.66 = bf16[2,32,1536]{2,1,0:T(8,128)(2,1)S(1)} collective-permute-done((bf16[2,32,1536]{2,1,0:T(8,128)(2,1)S(1)}, bf16[2,32,1536]{2,1,0:T(8,128)(2,1)S(1)}, u32[]{:S(2)}, u32[]{:S(2)}) %collective-permute-start.66) | collective-permute-done | bytes 196640 | tf_op jit(solution)/shard_map/ppermute | solution.py:66
  573.4 9.7 %collective-permute-done.54 = bf16[2,64,2048]{2,1,0:T(8,128)(2,1)S(1)} collective-permute-done((bf16[2,64,2048]{2,1,0:T(8,128)(2,1)S(1)}, bf16[2,64,2048]{2,1,0:T(8,128)(2,1)S(1)}, u32[]{:S(2)}, u32[]{:S(2)}) %collective-permute-start.54) | collective-permute-done | bytes 524320 | tf_op jit(solution)/shard_map/ppermute | solution.py:66
  (412 shorter events, 173.0 us)
Async XLA Ops:
  7.2 88.3 %all-gather.5.cloned.1.call-start = ((), (), s32[]{:S(2)}) async-start(), calls=%async_computation.4 | async-start | bytes 3342336 | tf_op jit(solution)/shard_map/all_gather | solution.py:444
  10.7 10.1 %collective-permute-start.5 = (bf16[2,32,512]{2,1,0:T(8,128)(2,1)S(1)}, bf16[2,32,512]{2,1,0:T(8,128)(2,1)S(1)}, u32[]{:S(2)}, u32[]{:S(2)}) collective-permute-start(bf16[2,32,512]{2,1,0:T(8,128)(2,1)S(1)} %get-tuple-element.124), channel_id=1, source_target_pairs={{0,72},{1,73},{2,74},{3,75},{4,76},{5,77},{6,78},{7,79},{8,64},{9,... | collective-permute-start | bytes 196616 | tf_op jit(solution)/shard_map/ppermute | solution.py:66
  24.1 177.2 %all-gather.7.cloned.1.call-start = ((), (), s32[]{:S(2)}) async-start(), calls=%async_computation.5 | async-start | bytes 10027008 | tf_op jit(solution)/shard_map/all_gather | solution.py:449
  24.7 7.4 %collective-permute-start.26 = (bf16[2,32,1536]{2,1,0:T(8,128)(2,1)S(1)}, bf16[2,32,1536]{2,1,0:T(8,128)(2,1)S(1)}, u32[]{:S(2)}, u32[]{:S(2)}) collective-permute-start(bf16[2,32,1536]{2,1,0:T(8,128)(2,1)S(1)} %pad_maximum_fusion.11), channel_id=1, source_target_pairs={{0,1},{1,0},{2,3},{3,2},{4,5},{5,4},{6,7},{7,6},{8,9},{9,8},{10,11... | collective-permute-start | bytes 589832 | tf_op jit(solution)/shard_map/ppermute | solution.py:66
  32.1 8.5 %collective-permute-start.27 = (bf16[2,32,1536]{2,1,0:T(8,128)(2,1)S(1)}, bf16[2,32,1536]{2,1,0:T(8,128)(2,1)S(1)}, u32[]{:S(2)}, u32[]{:S(2)}) collective-permute-start(bf16[2,32,1536]{2,1,0:T(8,128)(2,1)S(1)} %get-tuple-element.88), channel_id=1, source_target_pairs={{0,72},{1,73},{2,74},{3,75},{4,76},{5,77},{6,78},{7,79},{8,64},{9,... | collective-permute-start | bytes 589832 | tf_op jit(solution)/shard_map/ppermute | solution.py:66
  41.6 450.2 %reduce-scatter.3.cloned.1.call-start = ((), (), s32[]{:S(2)}) async-start(), calls=%async_computation.2 | async-start | bytes 3342336 | tf_op jit(solution)/shard_map/reduce_scatter | solution.py:547
  42.0 8.1 %collective-permute-start.9 = (f32[3,128]{1,0:T(4,128)S(1)}, f32[3,128]{1,0:T(4,128)S(1)}, u32[]{:S(2)}, u32[]{:S(2)}) collective-permute-start(f32[3,128]{1,0:T(4,128)S(1)} %get-tuple-element.128), channel_id=1, source_target_pairs={{0,8},{1,9},{2,10},{3,11},{4,12},{5,13},{6,14},{7,15},{8,0},{9,1},... | collective-permute-start | bytes 4616 | tf_op jit(solution)/shard_map/ppermute | solution.py:66
  42.1 9.3 %collective-permute-start.8 = (f32[3,128]{1,0:T(4,128)S(1)}, f32[3,128]{1,0:T(4,128)S(1)}, u32[]{:S(2)}, u32[]{:S(2)}) collective-permute-start(f32[3,128]{1,0:T(4,128)S(1)} %get-tuple-element.128), channel_id=1, source_target_pairs={{0,72},{1,73},{2,74},{3,75},{4,76},{5,77},{6,78},{7,79},{8,64},{9,... | collective-permute-start | bytes 4616 | tf_op jit(solution)/shard_map/ppermute | solution.py:66
  44.3 15.2 %collective-permute-start.2 = (bf16[128,2048]{1,0:T(8,128)(2,1)S(1)}, bf16[128,2048]{1,0:T(8,128)(2,1)S(1)}, u32[]{:S(2)}, u32[]{:S(2)}) collective-permute-start(bf16[128,2048]{1,0:T(8,128)(2,1)S(1)} %bitcast.440), channel_id=1, source_target_pairs={{0,64},{1,65},{2,66},{3,67},{4,68},{5,69},{6,70},{7,71},{8,72},{9,... | collective-permute-start | bytes 1572872 | tf_op jit(solution)/shard_map/ppermute | solution.py:66
  46.3 24.6 %collective-permute-start.1 = (bf16[128,2048]{1,0:T(8,128)(2,1)S(1)}, bf16[128,2048]{1,0:T(8,128)(2,1)S(1)}, u32[]{:S(2)}, u32[]{:S(2)}) collective-permute-start(bf16[128,2048]{1,0:T(8,128)(2,1)S(1)} %bitcast.441), channel_id=1, source_target_pairs={{0,8},{1,9},{2,10},{3,11},{4,12},{5,13},{6,14},{7,15},{8,0},{9,1},... | collective-permute-start | bytes 1572872 | tf_op jit(solution)/shard_map/ppermute | solution.py:66
  50.1 20.8 %collective-permute-start = (bf16[128,2048]{1,0:T(8,128)(2,1)S(1)}, bf16[128,2048]{1,0:T(8,128)(2,1)S(1)}, u32[]{:S(2)}, u32[]{:S(2)}) collective-permute-start(bf16[128,2048]{1,0:T(8,128)(2,1)S(1)} %bitcast.443), channel_id=1, source_target_pairs={{0,72},{1,73},{2,74},{3,75},{4,76},{5,77},{6,78},{7,79},{8,64},{9,... | collective-permute-start | bytes 1572872 | tf_op jit(solution)/shard_map/ppermute | solution.py:66
  51.4 21.0 %collective-permute-start.11 = (f32[4,3,128]{2,1,0:T(4,128)S(1)}, f32[4,3,128]{2,1,0:T(4,128)S(1)}, u32[]{:S(2)}, u32[]{:S(2)}) collective-permute-start(f32[4,3,128]{2,1,0:T(4,128)S(1)} %pad_maximum_fusion.13), channel_id=1, source_target_pairs={{0,1},{1,0},{2,3},{3,2},{4,5},{5,4},{6,7},{7,6},{8,9},{9,8},{10,11... | collective-permute-start | bytes 18440 | tf_op jit(solution)/shard_map/ppermute | solution.py:66
  72.4 19.9 %collective-permute-start.3 = (bf16[512,2048]{1,0:T(8,128)(2,1)}, bf16[512,2048]{1,0:T(8,128)(2,1)}, u32[]{:S(2)}, u32[]{:S(2)}) collective-permute-start(bf16[512,2048]{1,0:T(8,128)(2,1)} %pad_maximum_fusion.3), channel_id=1, source_target_pairs={{0,1},{1,0},{2,3},{3,2},{4,5},{5,4},{6,7},{7,6},{8,9},{9,8},{10,11... | collective-permute-start | bytes 6291464 | tf_op jit(solution)/shard_map/ppermute | solution.py:66
  72.4 8.0 %collective-permute-start.13 = (f32[2,128]{1,0:T(2,128)S(1)}, f32[2,128]{1,0:T(2,128)S(1)}, u32[]{:S(2)}, u32[]{:S(2)}) collective-permute-start(f32[2,128]{1,0:T(2,128)S(1)} %slice.471), channel_id=1, source_target_pairs={{0,4},{1,5},{2,6},{3,7},{4,0},{5,1},{6,2},{7,3},{8,12},{9,13},{10,... | collective-permute-start | bytes 3080 | tf_op jit(solution)/shard_map/ppermute | solution.py:66
  115.9 16.0 %collective-permute-start.34 = (bf16[128,2048]{1,0:T(8,128)(2,1)S(1)}, bf16[128,2048]{1,0:T(8,128)(2,1)S(1)}, u32[]{:S(2)}, u32[]{:S(2)}) collective-permute-start(bf16[128,2048]{1,0:T(8,128)(2,1)S(1)} %bitcast.456), channel_id=1, source_target_pairs={{0,64},{1,65},{2,66},{3,67},{4,68},{5,69},{6,70},{7,71},{8,72},{9,... | collective-permute-start | bytes 1572872 | tf_op jit(solution)/shard_map/ppermute | solution.py:66
  118.3 25.9 %collective-permute-start.33 = (bf16[128,2048]{1,0:T(8,128)(2,1)S(1)}, bf16[128,2048]{1,0:T(8,128)(2,1)S(1)}, u32[]{:S(2)}, u32[]{:S(2)}) collective-permute-start(bf16[128,2048]{1,0:T(8,128)(2,1)S(1)} %bitcast.457), channel_id=1, source_target_pairs={{0,8},{1,9},{2,10},{3,11},{4,12},{5,13},{6,14},{7,15},{8,0},{9,1},... | collective-permute-start | bytes 1572872 | tf_op jit(solution)/shard_map/ppermute | solution.py:66
  120.2 24.0 %collective-permute-start.32 = (bf16[128,2048]{1,0:T(8,128)(2,1)S(1)}, bf16[128,2048]{1,0:T(8,128)(2,1)S(1)}, u32[]{:S(2)}, u32[]{:S(2)}) collective-permute-start(bf16[128,2048]{1,0:T(8,128)(2,1)S(1)} %bitcast.458), channel_id=1, source_target_pairs={{0,72},{1,73},{2,74},{3,75},{4,76},{5,77},{6,78},{7,79},{8,64},{9,... | collective-permute-start | bytes 1572872 | tf_op jit(solution)/shard_map/ppermute | solution.py:66
  124.7 29.2 %collective-permute-start.19 = (bf16[128,2048]{1,0:T(8,128)(2,1)S(1)}, bf16[128,2048]{1,0:T(8,128)(2,1)S(1)}, u32[]{:S(2)}, u32[]{:S(2)}) collective-permute-start(bf16[128,2048]{1,0:T(8,128)(2,1)S(1)} %get-tuple-element.50), channel_id=1, source_target_pairs={{0,64},{1,65},{2,66},{3,67},{4,68},{5,69},{6,70},{7,71},{8,72},{9,... | collective-permute-start | bytes 1572872 | tf_op jit(solution)/shard_map/ppermute | solution.py:66
  125.3 30.0 %collective-permute-start.21 = (bf16[128,2048]{1,0:T(8,128)(2,1)S(1)}, bf16[128,2048]{1,0:T(8,128)(2,1)S(1)}, u32[]{:S(2)}, u32[]{:S(2)}) collective-permute-start(bf16[128,2048]{1,0:T(8,128)(2,1)S(1)} %get-tuple-element.51), channel_id=1, source_target_pairs={{0,72},{1,73},{2,74},{3,75},{4,76},{5,77},{6,78},{7,79},{8,64},{9,... | collective-permute-start | bytes 1572872 | tf_op jit(solution)/shard_map/ppermute | solution.py:66
  131.9 34.3 %collective-permute-start.20 = (bf16[128,2048]{1,0:T(8,128)(2,1)S(1)}, bf16[128,2048]{1,0:T(8,128)(2,1)S(1)}, u32[]{:S(2)}, u32[]{:S(2)}) collective-permute-start(bf16[128,2048]{1,0:T(8,128)(2,1)S(1)} %get-tuple-element.52), channel_id=1, source_target_pairs={{0,8},{1,9},{2,10},{3,11},{4,12},{5,13},{6,14},{7,15},{8,0},{9,1},... | collective-permute-start | bytes 1572872 | tf_op jit(solution)/shard_map/ppermute | solution.py:66
  144.4 51.4 %collective-permute-start.35 = (bf16[512,2048]{1,0:T(8,128)(2,1)S(1)}, bf16[512,2048]{1,0:T(8,128)(2,1)S(1)}, u32[]{:S(2)}, u32[]{:S(2)}) collective-permute-start(bf16[512,2048]{1,0:T(8,128)(2,1)S(1)} %pad_maximum_fusion.5), channel_id=1, source_target_pairs={{0,1},{1,0},{2,3},{3,2},{4,5},{5,4},{6,7},{7,6},{8,9},{9,8},{10,11... | collective-permute-start | bytes 6291464 | tf_op jit(solution)/shard_map/ppermute | solution.py:66
  168.6 16.2 %collective-permute-start.24 = (bf16[128,2048]{1,0:T(8,128)(2,1)S(1)}, bf16[128,2048]{1,0:T(8,128)(2,1)S(1)}, u32[]{:S(2)}, u32[]{:S(2)}) collective-permute-start(bf16[128,2048]{1,0:T(8,128)(2,1)S(1)} %get-tuple-element.27), channel_id=1, source_target_pairs={{0,64},{1,65},{2,66},{3,67},{4,68},{5,69},{6,70},{7,71},{8,72},{9,... | collective-permute-start | bytes 1572872 | tf_op jit(solution)/shard_map/ppermute | solution.py:66
  170.7 23.9 %collective-permute-start.23 = (bf16[128,2048]{1,0:T(8,128)(2,1)S(1)}, bf16[128,2048]{1,0:T(8,128)(2,1)S(1)}, u32[]{:S(2)}, u32[]{:S(2)}) collective-permute-start(bf16[128,2048]{1,0:T(8,128)(2,1)S(1)} %get-tuple-element.27), channel_id=1, source_target_pairs={{0,8},{1,9},{2,10},{3,11},{4,12},{5,13},{6,14},{7,15},{8,0},{9,1},... | collective-permute-start | bytes 1572872 | tf_op jit(solution)/shard_map/ppermute | solution.py:66
  172.3 22.8 %collective-permute-start.22 = (bf16[128,2048]{1,0:T(8,128)(2,1)S(1)}, bf16[128,2048]{1,0:T(8,128)(2,1)S(1)}, u32[]{:S(2)}, u32[]{:S(2)}) collective-permute-start(bf16[128,2048]{1,0:T(8,128)(2,1)S(1)} %get-tuple-element.27), channel_id=1, source_target_pairs={{0,72},{1,73},{2,74},{3,75},{4,76},{5,77},{6,78},{7,79},{8,64},{9,... | collective-permute-start | bytes 1572872 | tf_op jit(solution)/shard_map/ppermute | solution.py:66
  264.1 16.8 %collective-permute-start.37 = (bf16[128,2048]{1,0:T(8,128)(2,1)S(1)}, bf16[128,2048]{1,0:T(8,128)(2,1)S(1)}, u32[]{:S(2)}, u32[]{:S(2)}) collective-permute-start(bf16[128,2048]{1,0:T(8,128)(2,1)S(1)} %get-tuple-element.44), channel_id=1, source_target_pairs={{0,64},{1,65},{2,66},{3,67},{4,68},{5,69},{6,70},{7,71},{8,72},{9,... | collective-permute-start | bytes 1572872 | tf_op jit(solution)/shard_map/ppermute | solution.py:66
  265.7 24.9 %collective-permute-start.39 = (bf16[128,2048]{1,0:T(8,128)(2,1)S(1)}, bf16[128,2048]{1,0:T(8,128)(2,1)S(1)}, u32[]{:S(2)}, u32[]{:S(2)}) collective-permute-start(bf16[128,2048]{1,0:T(8,128)(2,1)S(1)} %get-tuple-element.45), channel_id=1, source_target_pairs={{0,72},{1,73},{2,74},{3,75},{4,76},{5,77},{6,78},{7,79},{8,64},{9,... | collective-permute-start | bytes 1572872 | tf_op jit(solution)/shard_map/ppermute | solution.py:66
  267.4 24.9 %collective-permute-start.38 = (bf16[128,2048]{1,0:T(8,128)(2,1)S(1)}, bf16[128,2048]{1,0:T(8,128)(2,1)S(1)}, u32[]{:S(2)}, u32[]{:S(2)}) collective-permute-start(bf16[128,2048]{1,0:T(8,128)(2,1)S(1)} %get-tuple-element.46), channel_id=1, source_target_pairs={{0,8},{1,9},{2,10},{3,11},{4,12},{5,13},{6,14},{7,15},{8,0},{9,1},... | collective-permute-start | bytes 1572872 | tf_op jit(solution)/shard_map/ppermute | solution.py:66
  269.7 32.1 %collective-permute-start.29 = (bf16[128,2048]{1,0:T(8,128)(2,1)S(1)}, bf16[128,2048]{1,0:T(8,128)(2,1)S(1)}, u32[]{:S(2)}, u32[]{:S(2)}) collective-permute-start(bf16[128,2048]{1,0:T(8,128)(2,1)S(1)} %get-tuple-element.47), channel_id=1, source_target_pairs={{0,64},{1,65},{2,66},{3,67},{4,68},{5,69},{6,70},{7,71},{8,72},{9,... | collective-permute-start | bytes 1572872 | tf_op jit(solution)/shard_map/ppermute | solution.py:66
  271.0 32.0 %collective-permute-start.31 = (bf16[128,2048]{1,0:T(8,128)(2,1)S(1)}, bf16[128,2048]{1,0:T(8,128)(2,1)S(1)}, u32[]{:S(2)}, u32[]{:S(2)}) collective-permute-start(bf16[128,2048]{1,0:T(8,128)(2,1)S(1)} %get-tuple-element.48), channel_id=1, source_target_pairs={{0,72},{1,73},{2,74},{3,75},{4,76},{5,77},{6,78},{7,79},{8,64},{9,... | collective-permute-start | bytes 1572872 | tf_op jit(solution)/shard_map/ppermute | solution.py:66
  280.9 33.0 %collective-permute-start.30 = (bf16[128,2048]{1,0:T(8,128)(2,1)S(1)}, bf16[128,2048]{1,0:T(8,128)(2,1)S(1)}, u32[]{:S(2)}, u32[]{:S(2)}) collective-permute-start(bf16[128,2048]{1,0:T(8,128)(2,1)S(1)} %get-tuple-element.49), channel_id=1, source_target_pairs={{0,8},{1,9},{2,10},{3,11},{4,12},{5,13},{6,14},{7,15},{8,0},{9,1},... | collective-permute-start | bytes 1572872 | tf_op jit(solution)/shard_map/ppermute | solution.py:66
  316.8 25.6 %collective-permute-start.42 = (bf16[128,2048]{1,0:T(8,128)(2,1)S(1)}, bf16[128,2048]{1,0:T(8,128)(2,1)S(1)}, u32[]{:S(2)}, u32[]{:S(2)}) collective-permute-start(bf16[128,2048]{1,0:T(8,128)(2,1)S(1)} %get-tuple-element.25), channel_id=1, source_target_pairs={{0,64},{1,65},{2,66},{3,67},{4,68},{5,69},{6,70},{7,71},{8,72},{9,... | collective-permute-start | bytes 1572872 | tf_op jit(solution)/shard_map/ppermute | solution.py:66
  318.0 24.4 %collective-permute-start.41 = (bf16[128,2048]{1,0:T(8,128)(2,1)S(1)}, bf16[128,2048]{1,0:T(8,128)(2,1)S(1)}, u32[]{:S(2)}, u32[]{:S(2)}) collective-permute-start(bf16[128,2048]{1,0:T(8,128)(2,1)S(1)} %get-tuple-element.25), channel_id=1, source_target_pairs={{0,8},{1,9},{2,10},{3,11},{4,12},{5,13},{6,14},{7,15},{8,0},{9,1},... | collective-permute-start | bytes 1572872 | tf_op jit(solution)/shard_map/ppermute | solution.py:66
  320.4 22.7 %collective-permute-start.40 = (bf16[128,2048]{1,0:T(8,128)(2,1)S(1)}, bf16[128,2048]{1,0:T(8,128)(2,1)S(1)}, u32[]{:S(2)}, u32[]{:S(2)}) collective-permute-start(bf16[128,2048]{1,0:T(8,128)(2,1)S(1)} %get-tuple-element.25), channel_id=1, source_target_pairs={{0,72},{1,73},{2,74},{3,75},{4,76},{5,77},{6,78},{7,79},{8,64},{9,... | collective-permute-start | bytes 1572872 | tf_op jit(solution)/shard_map/ppermute | solution.py:66
  378.8 165.8 %reduce-scatter.5.cloned.1.call-start = ((), (), s32[]{:S(2)}) async-start(), calls=%async_computation.3 | async-start | bytes 10027008 | tf_op jit(solution)/shard_map/reduce_scatter | solution.py:522
  440.5 24.2 %collective-permute-start.44 = (bf16[512,2048]{1,0:T(8,128)(2,1)}, bf16[512,2048]{1,0:T(8,128)(2,1)}, u32[]{:S(2)}, u32[]{:S(2)}) collective-permute-start(bf16[512,2048]{1,0:T(8,128)(2,1)} %slice.520), channel_id=1, source_target_pairs={{0,1},{1,0},{2,3},{3,2},{4,5},{5,4},{6,7},{7,6},{8,9},{9,8},{10,11... | collective-permute-start | bytes 6291464 | tf_op jit(solution)/shard_map/ppermute | solution.py:66
  460.5 11.1 %collective-permute-start.64 = (f32[2,128]{1,0:T(2,128)S(1)}, f32[2,128]{1,0:T(2,128)S(1)}, u32[]{:S(2)}, u32[]{:S(2)}) collective-permute-start(f32[2,128]{1,0:T(2,128)S(1)} %add_add_fusion.1), channel_id=1, source_target_pairs={{0,16},{1,17},{2,18},{3,19},{4,20},{5,21},{6,22},{7,23},{8,24},{9,... | collective-permute-start | bytes 3080 | tf_op jit(solution)/shard_map/ppermute | solution.py:66
  461.9 9.9 %collective-permute-start.63 = (f32[2,128]{1,0:T(2,128)S(1)}, f32[2,128]{1,0:T(2,128)S(1)}, u32[]{:S(2)}, u32[]{:S(2)}) collective-permute-start(f32[2,128]{1,0:T(2,128)S(1)} %add_add_fusion.1), channel_id=1, source_target_pairs={{0,32},{1,33},{2,34},{3,35},{4,36},{5,37},{6,38},{7,39},{8,40},{9,... | collective-permute-start | bytes 3080 | tf_op jit(solution)/shard_map/ppermute | solution.py:66
  464.4 7.4 %collective-permute-start.62 = (f32[2,128]{1,0:T(2,128)S(1)}, f32[2,128]{1,0:T(2,128)S(1)}, u32[]{:S(2)}, u32[]{:S(2)}) collective-permute-start(f32[2,128]{1,0:T(2,128)S(1)} %add_add_fusion.1), channel_id=1, source_target_pairs={{0,48},{1,49},{2,50},{3,51},{4,52},{5,53},{6,54},{7,55},{8,56},{9,... | collective-permute-start | bytes 3080 | tf_op jit(solution)/shard_map/ppermute | solution.py:66
  468.3 23.0 %collective-permute-start.45 = (bf16[128,2048]{1,0:T(8,128)(2,1)S(1)}, bf16[128,2048]{1,0:T(8,128)(2,1)S(1)}, u32[]{:S(2)}, u32[]{:S(2)}) collective-permute-start(bf16[128,2048]{1,0:T(8,128)(2,1)S(1)} %get-tuple-element.41), channel_id=1, source_target_pairs={{0,64},{1,65},{2,66},{3,67},{4,68},{5,69},{6,70},{7,71},{8,72},{9,... | collective-permute-start | bytes 1572872 | tf_op jit(solution)/shard_map/ppermute | solution.py:66
  468.4 22.9 %collective-permute-start.47 = (bf16[128,2048]{1,0:T(8,128)(2,1)S(1)}, bf16[128,2048]{1,0:T(8,128)(2,1)S(1)}, u32[]{:S(2)}, u32[]{:S(2)}) collective-permute-start(bf16[128,2048]{1,0:T(8,128)(2,1)S(1)} %get-tuple-element.42), channel_id=1, source_target_pairs={{0,72},{1,73},{2,74},{3,75},{4,76},{5,77},{6,78},{7,79},{8,64},{9,... | collective-permute-start | bytes 1572872 | tf_op jit(solution)/shard_map/ppermute | solution.py:66
  471.7 19.7 %collective-permute-start.46 = (bf16[128,2048]{1,0:T(8,128)(2,1)S(1)}, bf16[128,2048]{1,0:T(8,128)(2,1)S(1)}, u32[]{:S(2)}, u32[]{:S(2)}) collective-permute-start(bf16[128,2048]{1,0:T(8,128)(2,1)S(1)} %get-tuple-element.43), channel_id=1, source_target_pairs={{0,8},{1,9},{2,10},{3,11},{4,12},{5,13},{6,14},{7,15},{8,0},{9,1},... | collective-permute-start | bytes 1572872 | tf_op jit(solution)/shard_map/ppermute | solution.py:66
  492.8 7.6 %collective-permute-start.48 = (bf16[2,32,512]{2,1,0:T(8,128)(2,1)S(1)}, bf16[2,32,512]{2,1,0:T(8,128)(2,1)S(1)}, u32[]{:S(2)}, u32[]{:S(2)}) collective-permute-start(bf16[2,32,512]{2,1,0:T(8,128)(2,1)S(1)} %get-tuple-element.122), channel_id=1, source_target_pairs={{0,72},{1,73},{2,74},{3,75},{4,76},{5,77},{6,78},{7,79},{8,64},{9,... | collective-permute-start | bytes 196616 | tf_op jit(solution)/shard_map/ppermute | solution.py:66
  547.6 11.0 %collective-permute-start.65 = (bf16[2,32,1536]{2,1,0:T(8,128)(2,1)S(1)}, bf16[2,32,1536]{2,1,0:T(8,128)(2,1)S(1)}, u32[]{:S(2)}, u32[]{:S(2)}) collective-permute-start(bf16[2,32,1536]{2,1,0:T(8,128)(2,1)S(1)} %get-tuple-element.84), channel_id=1, source_target_pairs={{0,72},{1,73},{2,74},{3,75},{4,76},{5,77},{6,78},{7,79},{8,64},{9,... | collective-permute-start | bytes 589832 | tf_op jit(solution)/shard_map/ppermute | solution.py:66
  550.6 19.0 %collective-permute-start.53 = (bf16[64,2048]{1,0:T(8,128)(2,1)S(1)}, bf16[64,2048]{1,0:T(8,128)(2,1)S(1)}, u32[]{:S(2)}, u32[]{:S(2)}) collective-permute-start(bf16[64,2048]{1,0:T(8,128)(2,1)S(1)} %constant_dynamic-update-slice_fusion.85), channel_id=1, source_target_pairs={{2,0},{3,16},{6,1},{7,17},{10,8},{11,24},{14,9},{15,25},{18,2},{19... | collective-permute-start | bytes 786440 | tf_op jit(solution)/shard_map/ppermute | solution.py:66
  551.9 17.7 %collective-permute-start.52 = (bf16[64,2048]{1,0:T(8,128)(2,1)S(1)}, bf16[64,2048]{1,0:T(8,128)(2,1)S(1)}, u32[]{:S(2)}, u32[]{:S(2)}) collective-permute-start(bf16[64,2048]{1,0:T(8,128)(2,1)S(1)} %constant_dynamic-update-slice_fusion.85), channel_id=1, source_target_pairs={{0,0},{1,16},{4,1},{5,17},{8,8},{9,24},{12,9},{13,25},{16,2},{17,1... | collective-permute-start | bytes 786440 | tf_op jit(solution)/shard_map/ppermute | solution.py:66
  552.6 15.1 %collective-permute-start.67 = (bf16[2,32,1536]{2,1,0:T(8,128)(2,1)S(1)}, bf16[2,32,1536]{2,1,0:T(8,128)(2,1)S(1)}, u32[]{:S(2)}, u32[]{:S(2)}) collective-permute-start(bf16[2,32,1536]{2,1,0:T(8,128)(2,1)S(1)} %get-tuple-element.81), channel_id=1, source_target_pairs={{0,64},{1,65},{2,66},{3,67},{4,68},{5,69},{6,70},{7,71},{8,72},{9,... | collective-permute-start | bytes 589832 | tf_op jit(solution)/shard_map/ppermute | solution.py:66
  555.3 12.4 %collective-permute-start.66 = (bf16[2,32,1536]{2,1,0:T(8,128)(2,1)S(1)}, bf16[2,32,1536]{2,1,0:T(8,128)(2,1)S(1)}, u32[]{:S(2)}, u32[]{:S(2)}) collective-permute-start(bf16[2,32,1536]{2,1,0:T(8,128)(2,1)S(1)} %get-tuple-element.83), channel_id=1, source_target_pairs={{0,8},{1,9},{2,10},{3,11},{4,12},{5,13},{6,14},{7,15},{8,0},{9,1},... | collective-permute-start | bytes 589832 | tf_op jit(solution)/shard_map/ppermute | solution.py:66
  569.7 13.4 %collective-permute-start.54 = (bf16[2,64,2048]{2,1,0:T(8,128)(2,1)S(1)}, bf16[2,64,2048]{2,1,0:T(8,128)(2,1)S(1)}, u32[]{:S(2)}, u32[]{:S(2)}) collective-permute-start(bf16[2,64,2048]{2,1,0:T(8,128)(2,1)S(1)} %pad_maximum_fusion.9), channel_id=1, source_target_pairs={{0,64},{1,65},{2,66},{3,67},{4,68},{5,69},{6,70},{7,71},{8,72},{9,... | collective-permute-start | bytes 1572872 | tf_op jit(solution)/shard_map/ppermute | solution.py:66
  (62 other events, 454.2 us)
Sparse Core Ops, SparseCore 0:
  24.2 53.8 all-gather.4
  80.8 74.3 all-gather.6
  378.9 75.5 reduce-scatter.2
  457.9 86.6 reduce-scatter.4
